TPU v7x, 256 devices: a whole 4x4x8 slice. The times are simulated.
256 devices in a mesh: group: 32 (over z, y_lo, core), tp: 8 (over x, y_hi).
Axes of the slice: x: 4, y: 4 (y_hi: 2, y_lo: 2; y = y_hi * 2 + y_lo), z: 8, core: 2. Of those that a mesh axis runs over, the one named last changes fastest.
Arguments:
- prefill_queries: bfloat16 [32768, 8192], P(('group', 'tp')), may hold values from -160 to 160
- span_keys: bfloat16 [32768, 1024], P(('group', 'tp')), may hold values from -6 to 6
- span_values: bfloat16 [32768, 1024], P(('group', 'tp')), may hold values from -6 to 6
- prefix_keys: bfloat16 [32768, 1024], P(('group', 'tp')), may hold values from -6 to 6
- prefix_values: bfloat16 [32768, 1024], P(('group', 'tp')), may hold values from -6 to 6
- span_offsets: int32 [32], P('group'), may hold values from 0 to 1024, as said below
- prompt_lengths: int32 [32], P('group'), may hold values from 1 to 3072, as said below
- decode_queries: bfloat16 [1024, 2, 8192], P('group', None, 'tp'), may hold values from -160 to 160
- decode_new_keys: bfloat16 [1024, 2, 1024], P('group', None, 'tp'), may hold values from -6 to 6
- decode_new_values: bfloat16 [1024, 2, 1024], P('group', None, 'tp'), may hold values from -6 to 6
- cache_keys: bfloat16 [1024, 128, 1024], P('group', None, 'tp'), may hold values from -6 to 6
- cache_values: bfloat16 [1024, 128, 1024], P('group', None, 'tp'), may hold values from -6 to 6
- context_lengths: int32 [1024], P('group'), may hold values from 1 to 128
- placement: int32 [1024], replicated, may hold values from 0 to 31, as said below
- finished_lengths: int32 [1024], replicated, may hold values from 1 to 256, 131072 in all
- finished_keys: bfloat16 [1024, 256, 1024], P('group', 'tp'), may hold values from -6 to 6
- finished_values: bfloat16 [1024, 256, 1024], P('group', 'tp'), may hold values from -6 to 6
- arrival_queries: bfloat16 [2048, 2, 8192], P('group', None, 'tp'), may hold values from -160 to 160
- arrival_new_keys: bfloat16 [2048, 2, 1024], P('group', None, 'tp'), may hold values from -6 to 6
- arrival_new_values: bfloat16 [2048, 2, 1024], P('group', None, 'tp'), may hold values from -6 to 6
Outputs:
- prefill_out: bfloat16 [32768, 8192], P(('group', 'tp'))
- decode_out: bfloat16 [1024, 2, 8192], P('group', None, 'tp')
- arrival_out: bfloat16 [2048, 2, 8192], P('group', None, 'tp')
Inputs may be any that keep to these rules, and one draw needn't show every extreme that they name: `span_offsets`: multiples of 1024. `prompt_lengths`: each exceeds its group's span offset by 1 to 2048. `placement`: no group sends more than 2 of its finished prompts to one group; arrival slots without a prompt are ignored.
All inputs are finite; a program needn't handle non-finite values.
Results may differ from a plain program's by a relative error of at most 0.018.
Values may be sent and summed in bfloat16 or wider, within the bound.
A program may use at most 128 MiB of HBM per device.

v0:
```python
import math

import jax
import jax.numpy as jnp
from jax import lax
from jax.sharding import PartitionSpec as P

Q_HEADS = 64
KV_HEADS = 8
HEAD_DIM = 128
CAPACITY = 2


MASK_SCORE = -1e30


def decode_attend(queries, new_keys, new_values, cache_keys, cache_values, visible, filled):
    row_count, step_count, width = queries.shape
    kv_count = new_keys.shape[2] // HEAD_DIM
    group_size = width // HEAD_DIM // kv_count
    cache_count = cache_keys.shape[1]
    scale = 1.0 / math.sqrt(HEAD_DIM)
    query_heads = queries.reshape(row_count, step_count, kv_count, group_size, HEAD_DIM)
    key_cache = cache_keys.reshape(row_count, cache_count, kv_count, HEAD_DIM)
    value_cache = cache_values.reshape(row_count, cache_count, kv_count, HEAD_DIM)
    key_new = new_keys.reshape(row_count, step_count, kv_count, HEAD_DIM)
    value_new = new_values.reshape(row_count, step_count, kv_count, HEAD_DIM)
    cache_scores = (
        jnp.einsum("bskgd,blkd->bskgl", query_heads, key_cache, preferred_element_type=jnp.float32)
        * scale
    )
    new_scores = (
        jnp.einsum("bskgd,btkd->bskgt", query_heads, key_new, preferred_element_type=jnp.float32)
        * scale
    )
    cache_scores = jnp.where(visible[:, None, None, None, :], cache_scores, MASK_SCORE)
    step_ids = jnp.arange(step_count, dtype=jnp.int32)
    causal = step_ids[None, :] <= step_ids[:, None]
    new_scores = jnp.where(causal[None, :, None, None, :], new_scores, MASK_SCORE)
    row_max = jnp.maximum(jnp.max(cache_scores, axis=-1), jnp.max(new_scores, axis=-1))
    cache_weights = jnp.exp(cache_scores - row_max[..., None])
    new_weights = jnp.exp(new_scores - row_max[..., None])
    totals = jnp.sum(cache_weights, axis=-1) + jnp.sum(new_weights, axis=-1)
    mixed = jnp.einsum(
        "bskgl,blkd->bskgd",
        cache_weights.astype(jnp.bfloat16),
        value_cache,
        preferred_element_type=jnp.float32,
    )
    mixed = mixed + jnp.einsum(
        "bskgt,btkd->bskgd",
        new_weights.astype(jnp.bfloat16),
        value_new,
        preferred_element_type=jnp.float32,
    )
    mixed = mixed / totals[..., None]
    mixed = jnp.where(filled[:, None, None, None, None], mixed, 0.0)
    return mixed.reshape(row_count, step_count, width).astype(jnp.bfloat16)


def prefill_update(running, key_piece, value_piece, visible, query_heads):
    scale = 1.0 / math.sqrt(HEAD_DIM)
    piece_rows = key_piece.shape[0]
    key_heads = jnp.swapaxes(key_piece.reshape(piece_rows, KV_HEADS, HEAD_DIM), 0, 1)
    value_heads = jnp.swapaxes(value_piece.reshape(piece_rows, KV_HEADS, HEAD_DIM), 0, 1)

    def per_head(operands):
        query_one, key_one, value_one, max_one, total_one, accum_one = operands
        scores = (
            jnp.einsum("gid,jd->gij", query_one, key_one, preferred_element_type=jnp.float32)
            * scale
        )
        scores = jnp.where(visible[None], scores, MASK_SCORE)
        new_max = jnp.maximum(max_one, jnp.max(scores, axis=-1))
        rescale = jnp.exp(max_one - new_max)
        weights = jnp.exp(scores - new_max[..., None])
        total_one = total_one * rescale + jnp.sum(weights, axis=-1)
        accum_one = accum_one * rescale[..., None] + jnp.einsum(
            "gij,jd->gid",
            weights.astype(jnp.bfloat16),
            value_one,
            preferred_element_type=jnp.float32,
        )
        return (new_max, total_one, accum_one)

    row_max, totals, accum = running
    return lax.map(per_head, (query_heads, key_heads, value_heads, row_max, totals, accum))


def local(
    prefill_queries,
    span_keys,
    span_values,
    prefix_keys,
    prefix_values,
    span_offsets,
    prompt_lengths,
    decode_queries,
    decode_new_keys,
    decode_new_values,
    cache_keys,
    cache_values,
    context_lengths,
    placement,
    finished_lengths,
    finished_keys,
    finished_values,
    arrival_queries,
    arrival_new_keys,
    arrival_new_values,
):
    group_count = lax.axis_size("group")
    group_index = lax.axis_index("group")
    tp_index = lax.axis_index("tp")
    finished_count = finished_keys.shape[0]
    local_len = finished_keys.shape[1]
    kv_width = finished_keys.shape[2]
    routes = placement.reshape(group_count, finished_count)
    finished_ids = jnp.arange(finished_count, dtype=jnp.int32)
    earlier = finished_ids[None, :] < finished_ids[:, None]
    arrival_rank = jnp.sum(
        ((routes[:, :, None] == routes[:, None, :]) & earlier[None]).astype(jnp.int32), axis=2
    )
    slot_ids = jnp.arange(CAPACITY, dtype=jnp.int32)
    dest_ids = jnp.arange(group_count, dtype=jnp.int32)
    own_routes = lax.dynamic_slice_in_dim(routes, group_index, 1, 0)[0]
    own_rank = lax.dynamic_slice_in_dim(arrival_rank, group_index, 1, 0)[0]
    selector = (
        (own_routes[None, None, :] == dest_ids[:, None, None])
        & (own_rank[None, None, :] == slot_ids[None, :, None])
    ).astype(jnp.bfloat16)
    bucket_keys = jnp.einsum(
        "dcf,fx->dcx",
        selector,
        finished_keys.reshape(finished_count, local_len * kv_width),
        preferred_element_type=jnp.float32,
    ).astype(jnp.bfloat16)
    bucket_values = jnp.einsum(
        "dcf,fx->dcx",
        selector,
        finished_values.reshape(finished_count, local_len * kv_width),
        preferred_element_type=jnp.float32,
    ).astype(jnp.bfloat16)
    bucket_keys = bucket_keys.reshape(group_count, CAPACITY, local_len, kv_width)
    bucket_values = bucket_values.reshape(group_count, CAPACITY, local_len, kv_width)
    got_keys, got_values = (
        lax.all_to_all(
            lax.all_to_all(bucket_keys, "group", split_axis=0, concat_axis=0, tiled=True),
            "tp",
            split_axis=3,
            concat_axis=2,
            tiled=True,
        ),
        lax.all_to_all(
            lax.all_to_all(bucket_values, "group", split_axis=0, concat_axis=0, tiled=True),
            "tp",
            split_axis=3,
            concat_axis=2,
            tiled=True,
        ),
    )
    rows_local = prefill_queries.shape[0]
    offset = span_offsets[0]
    length = prompt_lengths[0]
    span_index = tp_index * rows_local + jnp.arange(rows_local, dtype=jnp.int32)
    group_size = Q_HEADS // KV_HEADS
    query_heads = prefill_queries.reshape(rows_local, KV_HEADS, group_size, HEAD_DIM).transpose(
        1, 2, 0, 3
    )
    running = (
        jnp.full((KV_HEADS, group_size, rows_local), MASK_SCORE, jnp.float32),
        jnp.zeros((KV_HEADS, group_size, rows_local), jnp.float32),
        jnp.zeros((KV_HEADS, group_size, rows_local, HEAD_DIM), jnp.float32),
    )
    pieces = (
        lax.all_gather(prefix_keys, "tp", axis=0, tiled=True),
        lax.all_gather(prefix_values, "tp", axis=0, tiled=True),
    )
    positions = jnp.arange(pieces[0].shape[0], dtype=jnp.int32)
    visible = jnp.broadcast_to((positions < offset)[None, :], (rows_local, positions.shape[0]))
    running = prefill_update(running, pieces[0], pieces[1], visible, query_heads)
    pieces = (
        lax.all_gather(span_keys, "tp", axis=0, tiled=True),
        lax.all_gather(span_values, "tp", axis=0, tiled=True),
    )
    positions = jnp.arange(pieces[0].shape[0], dtype=jnp.int32)
    visible = positions[None, :] <= span_index[:, None]
    running = prefill_update(running, pieces[0], pieces[1], visible, query_heads)
    row_max, totals, accum = running
    mixed = (
        (accum / totals[..., None]).transpose(2, 0, 1, 3).reshape(rows_local, Q_HEADS * HEAD_DIM)
    )
    filled_rows = offset + span_index < length
    prefill_out = jnp.where(filled_rows[:, None], mixed, 0.0).astype(jnp.bfloat16)
    cache_ids = jnp.arange(cache_keys.shape[1], dtype=jnp.int32)
    resident_visible = cache_ids[None, :] < context_lengths[:, None]
    resident_filled = jnp.ones((decode_queries.shape[0],), jnp.bool_)
    decode_out = decode_attend(
        decode_queries,
        decode_new_keys,
        decode_new_values,
        cache_keys,
        cache_values,
        resident_visible,
        resident_filled,
    )
    arrival_count = group_count * CAPACITY
    matched = (routes == group_index)[:, None, :] & (
        arrival_rank[:, None, :] == slot_ids[None, :, None]
    )
    prompt_lens = finished_lengths.reshape(group_count, finished_count)
    slot_len = jnp.sum(jnp.where(matched, prompt_lens[:, None, :], 0), axis=-1).reshape(
        arrival_count
    )
    slot_filled = jnp.any(matched, axis=-1).reshape(arrival_count)
    full_len = got_keys.shape[2]
    arrival_keys = got_keys.reshape(arrival_count, full_len, got_keys.shape[3])
    arrival_values = got_values.reshape(arrival_count, full_len, got_values.shape[3])
    arrival_visible = jnp.arange(full_len, dtype=jnp.int32)[None, :] < slot_len[:, None]
    arrival_out = decode_attend(
        arrival_queries,
        arrival_new_keys,
        arrival_new_values,
        arrival_keys,
        arrival_values,
        arrival_visible,
        slot_filled,
    )
    return (prefill_out, decode_out, arrival_out)


def solution(mesh):
    placed = (
        P(("group", "tp"), None),
        P(("group", "tp"), None),
        P(("group", "tp"), None),
        P(("group", "tp"), None),
        P(("group", "tp"), None),
        P("group"),
        P("group"),
        P("group", None, "tp"),
        P("group", None, "tp"),
        P("group", None, "tp"),
        P("group", None, "tp"),
        P("group", None, "tp"),
        P("group"),
        P(),
        P(),
        P("group", "tp", None),
        P("group", "tp", None),
        P("group", None, "tp"),
        P("group", None, "tp"),
        P("group", None, "tp"),
    )
    return jax.shard_map(
        local,
        mesh=mesh,
        in_specs=placed,
        out_specs=(P(("group", "tp"), None), P("group", None, "tp"), P("group", None, "tp")),
        check_vma=False,
    )
```

profile of v0, /device:TPU:32, one launch (start us, length us, event | category | flops | bytes accessed | tf_op | source)
XLA Modules:
  0.0 535.7 jit_solution(4285502483796860080)
XLA Ops:
  17.9 9.9 %all-to-all-start.2 = ((bf16[32,2,32,1024]{3,2,1,0:T(8,128)(2,1)}), bf16[32,2,32,1024]{3,2,1,0:T(8,128)(2,1)}, u32[]{:S(2)}, u32[]{:S(2)}) async-start(bf16[32,2,32,1024]{3,2,1,0:T(8,128)(2,1)} %copy.75), calls=%async_computation.2 | async-start | bytes 8388608 | tf_op jit(solution)/shard_map/all_to_all | solution.py:148
  38.7 84.7 %all-to-all-done.2 = bf16[32,2,32,1024]{3,2,1,0:T(8,128)(2,1)} async-done(((bf16[32,2,32,1024]{3,2,1,0:T(8,128)(2,1)}), bf16[32,2,32,1024]{3,2,1,0:T(8,128)(2,1)}, u32[]{:S(2)}, u32[]{:S(2)}) %all-to-all-start.2) | async-done | bytes 4194336 | tf_op jit(solution)/shard_map/all_to_all | solution.py:148
  123.3 5.9 %all-to-all-start = ((bf16[32,2,32,1024]{3,2,1,0:T(8,128)(2,1)}), bf16[32,2,32,1024]{3,2,1,0:T(8,128)(2,1)}, u32[]{:S(2)}, u32[]{:S(2)}) async-start(bf16[32,2,32,1024]{3,2,1,0:T(8,128)(2,1)} %copy.71), calls=%async_computation | async-start | bytes 8388608 | tf_op jit(solution)/shard_map/all_to_all | solution.py:155
  130.2 10.0 %all-gather.11.cloned.1.call-start = ((), (), s32[]{:S(2)}) async-start(), calls=%async_computation.7 | async-start | bytes 2359296 | tf_op jit(solution)/shard_map/all_gather | solution.py:184
  157.7 23.2 %copy.76 = bf16[32,2,32,1024]{2,0,1,3:T(8,128)(2,1)} copy(bf16[32,2,32,1024]{3,2,1,0:T(8,128)(2,1)} %all-to-all-done.2) | data formatting | bytes 8388608 | tf_op jit(solution)/shard_map/all_to_all | solution.py:148
  180.8 18.7 %reshape.411 = bf16[8,2,131072]{2,1,0:T(2,128)(2,1)} reshape(bf16[1024,2,32,32]{3,2,1,0:T(8,128)(2,1)} %bitcast.279) | data formatting | bytes 8388608
  199.5 25.3 %all-to-all-done = bf16[32,2,32,1024]{3,2,1,0:T(8,128)(2,1)} async-done(((bf16[32,2,32,1024]{3,2,1,0:T(8,128)(2,1)}), bf16[32,2,32,1024]{3,2,1,0:T(8,128)(2,1)}, u32[]{:S(2)}, u32[]{:S(2)}) %all-to-all-start) | async-done | bytes 4194336 | tf_op jit(solution)/shard_map/all_to_all | solution.py:155
  224.9 6.6 %all-to-all-start.3 = ((bf16[8,2,131072]{2,1,0:T(2,128)(2,1)}), bf16[8,2,131072]{2,1,0:T(2,128)(2,1)}, u32[]{:S(2)}, u32[]{:S(2)}) async-start(bf16[8,2,131072]{2,1,0:T(2,128)(2,1)} %reshape.411), calls=%async_computation.3 | async-start | bytes 8388608 | tf_op jit(solution)/shard_map/all_to_all | solution.py:147
  234.0 45.4 %while.28 = (s32[]{:T(128)}, f32[8,8,128]{2,1,0:T(8,128)S(1)}, f32[8,8,128]{2,1,0:T(8,128)S(1)}, f32[8,8,128,128]{3,2,1,0:T(8,128)}, bf16[8,8,128,128]{3,2,1,0:T...) while((s32[]{:T(128)}, f32[8,8,128]{2,1,0:T(8,128)S(1)}, ...), condition=%wide.region_3.4_spmd.clone, body=%wide.region_0.3_spmd.clone.sunk | while | flops 548541440 | bytes 13948001 | solution.py:87
  279.5 23.2 %copy.72 = bf16[32,2,32,1024]{2,0,1,3:T(8,128)(2,1)} copy(bf16[32,2,32,1024]{3,2,1,0:T(8,128)(2,1)} %all-to-all-done) | data formatting | bytes 8388608 | tf_op jit(solution)/shard_map/all_to_all | solution.py:155
  302.7 18.7 %reshape.413 = bf16[8,2,131072]{2,1,0:T(2,128)(2,1)} reshape(bf16[1024,2,32,32]{3,2,1,0:T(8,128)(2,1)} %bitcast.280) | data formatting | bytes 8388608
  321.4 7.2 %all-to-all-start.1 = ((bf16[8,2,131072]{2,1,0:T(2,128)(2,1)}), bf16[8,2,131072]{2,1,0:T(2,128)(2,1)}, u32[]{:S(2)}, u32[]{:S(2)}) async-start(bf16[8,2,131072]{2,1,0:T(2,128)(2,1)} %reshape.413), calls=%async_computation.1 | async-start | bytes 8388608 | tf_op jit(solution)/shard_map/all_to_all | solution.py:154
  328.6 70.9 %all-gather.11.cloned.1.call-done = bf16[1024,1024]{0,1:T(8,128)(2,1)} async-done(((bf16[128,1024]{0,1:T(8,128)(2,1)}), bf16[1024,1024]{0,1:T(8,128)(2,1)}) %all-gather.11.cloned.1.call-update) | async-done | bytes 2097168 | tf_op jit(solution)/shard_map/all_gather | solution.py:184
  401.9 50.9 %while.29 = (s32[]{:T(128)}, f32[8,8,128]{2,1,0:T(8,128)S(1)}, f32[8,8,128,128]{3,2,1,0:T(8,128)}, f32[8,8,128]{2,1,0:T(8,128)S(1)}, f32[8,8,128]{2,1,0:T(8,128)...) while((s32[]{:T(128)}, f32[8,8,128]{2,1,0:T(8,128)S(1)}, ...), condition=%wide.region_7.8_spmd.clone, body=%wide.region_4.7_spmd.clone.sunk | while | flops 548802560 | bytes 15002229 | solution.py:87
  416.6 3.2 fusion.156
  423.0 3.2 fusion.156
  435.7 3.2 fusion.156
  448.4 3.2 fusion.156
  457.0 3.2 fusion.64
  460.2 12.4 %reshape.412 = bf16[1024,2,32,32]{3,2,1,0:T(8,128)(2,1)} reshape(bf16[8,2,131072]{2,1,0:T(2,128)(2,1)} %all-to-all-done.3) | data formatting | bytes 8388608
  472.7 17.5 %copy.77 = bf16[32,2,32,8,128]{4,2,3,1,0:T(8,128)(2,1)} copy(bf16[32,2,32,8,128]{2,0,1,4,3:T(8,128)(2,1)} %bitcast.281) | data formatting | bytes 8388608 | tf_op jit(solution)/shard_map/all_to_all | solution.py:147
  490.1 3.5 fusion.121
  494.7 12.7 %reshape.414 = bf16[1024,2,32,32]{3,2,1,0:T(8,128)(2,1)} reshape(bf16[8,2,131072]{2,1,0:T(2,128)(2,1)} %all-to-all-done.1) | data formatting | bytes 8388608
  507.4 17.5 %copy.73 = bf16[32,2,32,8,128]{4,2,3,1,0:T(8,128)(2,1)} copy(bf16[32,2,32,8,128]{2,0,1,4,3:T(8,128)(2,1)} %bitcast.282) | data formatting | bytes 8388608 | tf_op jit(solution)/shard_map/all_to_all | solution.py:154
  (180 shorter events, 135.5 us)
Async XLA Ops:
  7.2 138.4 %copy-start = (bf16[32,128,128]{2,1,0:T(8,128)(2,1)S(1)}, bf16[32,128,128]{2,1,0:T(8,128)(2,1)}, u32[]{:S(2)}) copy-start(bf16[32,128,128]{2,1,0:T(8,128)(2,1)} %param.34) | copy-start | bytes 3145732
  17.9 10.0 %copy-start.3 = (bf16[128,1024]{1,0:T(8,128)(2,1)S(1)}, bf16[128,1024]{1,0:T(8,128)(2,1)}, u32[]{:S(2)}) copy-start(bf16[128,1024]{1,0:T(8,128)(2,1)} %param.27) | copy-start | bytes 786436
  17.9 10.9 %copy-start.4 = (bf16[128,1024]{1,0:T(8,128)(2,1)S(1)}, bf16[128,1024]{1,0:T(8,128)(2,1)}, u32[]{:S(2)}) copy-start(bf16[128,1024]{1,0:T(8,128)(2,1)} %param.28) | copy-start | bytes 786436
  17.9 105.5 %all-to-all-start.2 = ((bf16[32,2,32,1024]{3,2,1,0:T(8,128)(2,1)}), bf16[32,2,32,1024]{3,2,1,0:T(8,128)(2,1)}, u32[]{:S(2)}, u32[]{:S(2)}) async-start(bf16[32,2,32,1024]{3,2,1,0:T(8,128)(2,1)} %copy.75), calls=%async_computation.2 | async-start | bytes 8388608 | tf_op jit(solution)/shard_map/all_to_all | solution.py:148
  27.8 203.7 %all-gather.5.cloned.1.call-start = ((), (), s32[]{:S(2)}) async-start(), calls=%async_computation.4 | async-start | bytes 2359296 | tf_op jit(solution)/shard_map/all_gather | solution.py:176
  28.7 202.8 %all-gather.7.cloned.1.call-start = ((), (), s32[]{:S(2)}) async-start(), calls=%async_computation.5 | async-start | bytes 2359296 | tf_op jit(solution)/shard_map/all_gather | solution.py:177
  38.7 90.7 %copy-start.5 = (bf16[128,1024]{1,0:T(8,128)(2,1)S(1)}, bf16[128,1024]{1,0:T(8,128)(2,1)}, u32[]{:S(2)}) copy-start(bf16[128,1024]{1,0:T(8,128)(2,1)} %param.25) | copy-start | bytes 786436
  38.7 101.6 %copy-start.6 = (bf16[128,1024]{1,0:T(8,128)(2,1)S(1)}, bf16[128,1024]{1,0:T(8,128)(2,1)}, u32[]{:S(2)}) copy-start(bf16[128,1024]{1,0:T(8,128)(2,1)} %param.26) | copy-start | bytes 786436
  38.7 102.5 %copy-start.8 = (s32[1024]{0:T(1024)S(1)}, s32[1024]{0:T(1024)}, u32[]{:S(2)}) copy-start(s32[1024]{0:T(1024)} %param.38) | copy-start | bytes 12292
  38.7 105.4 %copy-start.9 = (s32[32]{0:T(128)S(1)}, s32[32]{0:T(128)}, u32[]{:S(2)}) copy-start(s32[32]{0:T(128)} %param.36) | copy-start | bytes 388
  123.3 101.5 %all-to-all-start = ((bf16[32,2,32,1024]{3,2,1,0:T(8,128)(2,1)}), bf16[32,2,32,1024]{3,2,1,0:T(8,128)(2,1)}, u32[]{:S(2)}, u32[]{:S(2)}) async-start(bf16[32,2,32,1024]{3,2,1,0:T(8,128)(2,1)} %copy.71), calls=%async_computation | async-start | bytes 8388608 | tf_op jit(solution)/shard_map/all_to_all | solution.py:155
  129.3 199.3 %all-gather.9.cloned.1.call-start = ((), (), s32[]{:S(2)}) async-start(), calls=%async_computation.6 | async-start | bytes 2359296 | tf_op jit(solution)/shard_map/all_gather | solution.py:183
  130.2 19.3 %copy-start.2 = (bf16[128,8192]{1,0:T(8,128)(2,1)S(1)}, bf16[128,8192]{1,0:T(8,128)(2,1)}, u32[]{:S(2)}) copy-start(bf16[128,8192]{1,0:T(8,128)(2,1)} %param.24) | copy-start | bytes 6291460
  130.2 269.2 %all-gather.11.cloned.1.call-start = ((), (), s32[]{:S(2)}) async-start(), calls=%async_computation.7 | async-start | bytes 2359296 | tf_op jit(solution)/shard_map/all_gather | solution.py:184
  144.0 4.5 copy-start.11
  149.5 6.9 %copy-start.10 = (bf16[64,2,128]{2,1,0:T(2,128)(2,1)S(1)}, bf16[64,2,128]{2,1,0:T(2,128)(2,1)}, u32[]{:S(2)}) copy-start(bf16[64,2,128]{2,1,0:T(2,128)(2,1)} %param.42) | copy-start | bytes 98308
  224.9 96.5 %all-to-all-start.3 = ((bf16[8,2,131072]{2,1,0:T(2,128)(2,1)}), bf16[8,2,131072]{2,1,0:T(2,128)(2,1)}, u32[]{:S(2)}, u32[]{:S(2)}) async-start(bf16[8,2,131072]{2,1,0:T(2,128)(2,1)} %reshape.411), calls=%async_computation.3 | async-start | bytes 8388608 | tf_op jit(solution)/shard_map/all_to_all | solution.py:147
  321.4 173.3 %all-to-all-start.1 = ((bf16[8,2,131072]{2,1,0:T(2,128)(2,1)}), bf16[8,2,131072]{2,1,0:T(2,128)(2,1)}, u32[]{:S(2)}, u32[]{:S(2)}) async-start(bf16[8,2,131072]{2,1,0:T(2,128)(2,1)} %reshape.413), calls=%async_computation.1 | async-start | bytes 8388608 | tf_op jit(solution)/shard_map/all_to_all | solution.py:154
  490.1 4.2 copy-start.7
  524.9 3.9 copy-start.1
Sparse Core Ops, SparseCore 0:
  31.7 73.8 all-gather.4
  108.1 78.5 all-gather.6
  189.2 82.2 all-gather.8
  273.8 125.5 all-gather.10
where the time goes:
time: 547 us; the launch traced here: 536 us
  waiting for transfers between devices  181 us (33%)
  local copies, waits for them, and re-layouts  179 us (33%)
  matrix products  91.7 us (17%)
  starting transfers between devices  39.8 us (7%)
  other arithmetic  27.4 us (5%)
  between operations  15.9 us (3%)
    all_to_all x1, waiting for transfers between devices, local(): lax.all_to_all(bucket_keys, 'group', split_axis=0, concat_axis=0, tiled=T...  84.7 us
    unnamed x36, local copies, waits for them, and re-layouts  76.4 us
    all_gather x1, waiting for transfers between devices, local(): lax.all_gather(span_values, 'tp', axis=0, tiled=True)  70.9 us
    dot_general x16, matrix products, per_head(): jnp.einsum('gij,jd->gid', weights.astype(jnp.bfloat16), value_one, prefer...  48.1 us
    dot_general x16, matrix products, per_head(): jnp.einsum('gid,jd->gij', query_one, key_one, preferred_element_type=jnp....  28.9 us
    all_to_all x1, waiting for transfers between devices, local(): lax.all_to_all(bucket_values, 'group', split_axis=0, concat_axis=0, tiled...  25.3 us
    all_to_all x1, local copies, waits for them, and re-layouts, local(): lax.all_to_all(bucket_keys, 'group', split_axis=0, concat_axis=0, tiled=T...  23.2 us
    all_to_all x1, local copies, waits for them, and re-layouts, local(): lax.all_to_all(bucket_values, 'group', split_axis=0, concat_axis=0, tiled...  23.2 us
  transfers between devices with their start and end apart: 8, of which 3 were waited for; matrix products, arithmetic and copies ran while one was open for 47% of the time, Pallas kernels for 0%

commit v1 on v0

v1 whole, which is shorter than its diff:
```python
import functools
import math

import jax
import jax.numpy as jnp
from jax import lax
from jax.experimental import pallas as pl
from jax.experimental.pallas import tpu as pltpu
from jax.sharding import PartitionSpec as P

KV_HEADS = 8
GROUP_SIZE = 8
HEAD_DIM = 128
CAPACITY = 2
STEPS = 2
ROWS16 = GROUP_SIZE * STEPS
MESH = pl.DeviceIdType.MESH
NEG = -1e30
RATE = math.log2(math.e) / math.sqrt(HEAD_DIM)
X_CHIPS = 4


def dot_t(a, b):
    return lax.dot_general(a, b, (((1,), (1,)), ((), ())), preferred_element_type=jnp.float32)


def dot_n(a, b):
    return lax.dot_general(a, b, (((1,), (0,)), ((), ())), preferred_element_type=jnp.float32)


def spread(row, reps):
    n = row.shape[1]
    owner = lax.broadcasted_iota(jnp.int32, (n * reps, n), 0) // reps
    lane = lax.broadcasted_iota(jnp.int32, (n * reps, n), 1)
    return jnp.sum(jnp.where(owner == lane, row, 0.0), axis=1, keepdims=True)


def new_scores(q3, nk):
    shape = q3.shape[:2] + (1,)
    step = lax.broadcasted_iota(jnp.int32, shape, 1) % STEPS
    first = jnp.sum(q3 * nk[0], axis=2, keepdims=True)
    second = jnp.sum(q3 * nk[1], axis=2, keepdims=True)
    return first, jnp.where(step >= 1, second, NEG)


def body(
    n_groups,
    n_tp,
    pq,
    sk,
    sv,
    pk,
    pv,
    span_offset,
    prompt_length,
    dq,
    dnk,
    dnv,
    ck,
    cv,
    context,
    routes,
    lengths,
    fk,
    fv,
    msg,
    p_out,
    d_out,
    a_out,
    kv,
    q_s,
    ck_s,
    cv_s,
    fk_s,
    fv_s,
    rm,
    aq,
    po,
    ro,
    ps,
    rs,
    sel,
    bias,
    ret,
    ao,
    load_kv,
    load_big,
    x_send,
    x_recv,
    m_send,
    m_recv,
    q_send,
    q_recv,
    o_send,
    o_recv,
    s_send,
    s_recv,
    b_send,
    b_recv,
    own_sem,
):
    g = lax.axis_index("group")
    t = lax.axis_index("tp")
    x, yh = t // 2, t % 2
    right = ((x + 1) % X_CHIPS) * 2 + yh
    left = ((x + X_CHIPS - 1) % X_CHIPS) * 2 + yh
    partner = x * 2 + (1 - yh)
    right_x = (x + 1) % X_CHIPS
    left_x = (x + X_CHIPS - 1) % X_CHIPS
    far_x = (x + 2) % X_CHIPS
    n_prompts = routes.shape[1]
    a_rows = n_prompts * ROWS16
    quads = n_prompts // 4
    rows = pq.shape[0]

    arrays = (pk, sk, pv, sv)

    def kv_load(h, a):
        cols = pl.ds(pl.multiple_of(h * HEAD_DIM, HEAD_DIM), HEAD_DIM)
        return pltpu.make_async_copy(arrays[a].at[:, cols], kv.at[h, a, t], load_kv.at[h, a])

    def start_loads(h, c):
        for a in range(4):
            kv_load(h, a).start()
        return c

    lax.fori_loop(0, KV_HEADS, start_loads, 0)
    big = [
        pltpu.make_async_copy(src, dst, load_big.at[i])
        for i, (src, dst) in enumerate(
            ((ck, ck_s), (cv, cv_s), (pq, q_s), (fk, fk_s), (fv, fv_s))
        )
    ]
    for copy in big:
        copy.start()
    own_msg = pltpu.make_async_copy(msg.at[g], rm.at[g], own_sem)
    own_msg.start()

    barrier = pltpu.get_barrier_semaphore()

    def greet_group(k, c):
        pl.semaphore_signal(
            barrier, inc=1, device_id={"group": (g + k) % n_groups}, device_id_type=MESH
        )
        return c

    def greet_tp(k, c):
        pl.semaphore_signal(barrier, inc=1, device_id={"tp": (t + k) % n_tp}, device_id_type=MESH)
        return c

    lax.fori_loop(1, n_groups, greet_group, 0)
    lax.fori_loop(1, n_tp, greet_tp, 0)
    pl.semaphore_wait(barrier, n_groups - 1 + n_tp - 1)

    def to_tp(src, dst, kind, h, peer):
        return pltpu.make_async_remote_copy(
            src_ref=src,
            dst_ref=dst,
            send_sem=x_send.at[h, kind],
            recv_sem=x_recv.at[h, kind],
            device_id={"tp": peer},
            device_id_type=MESH,
        )

    def block_copy(h, block, kind, peer):
        ref = kv.at[h, :, block]
        return to_tp(ref, ref, kind, h, peer)

    def pair_copy(h, arr, xs, kind, peer):
        ref = kv.at[h, pl.ds(arr, 2), pl.ds(xs * 2, 2)]
        return to_tp(ref, ref, kind, h, peer)

    def stage1(h):
        for a in range(4):
            kv_load(h, a).wait()
        block_copy(h, t, 0, partner).start()
        block_copy(h, t, 1, right).start()
        block_copy(h, t, 2, left).start()

    def stage2(h):
        block_copy(h, partner, 0, partner).wait_recv()
        block_copy(h, partner, 3, right).start()
        block_copy(h, partner, 4, left).start()

    def stage3(h):
        block_copy(h, left_x * 2 + yh, 1, right).wait_recv()
        block_copy(h, left_x * 2 + (1 - yh), 3, right).wait_recv()
        pair_copy(h, 0, left_x, 5, right).start()
        block_copy(h, right_x * 2 + yh, 2, left).wait_recv()
        block_copy(h, right_x * 2 + (1 - yh), 4, left).wait_recv()
        pair_copy(h, 2, right_x, 6, left).start()

    def stage4(h):
        pair_copy(h, 0, far_x, 5, right).wait_recv()
        pair_copy(h, 2, far_x, 6, left).wait_recv()

    def msg_copy(k):
        peer = (g + k) % n_groups
        return pltpu.make_async_remote_copy(
            src_ref=msg.at[peer],
            dst_ref=rm.at[g],
            send_sem=m_send.at[k],
            recv_sem=m_recv.at[g],
            device_id={"group": peer},
            device_id_type=MESH,
        )

    def msg_wait(k):
        peer = (g + k) % n_groups
        pltpu.make_async_remote_copy(
            src_ref=rm.at[peer],
            dst_ref=rm.at[peer],
            send_sem=m_send.at[k],
            recv_sem=m_recv.at[peer],
            device_id={"group": peer},
            device_id_type=MESH,
        ).wait_recv()

    def send_msg(k, c):
        msg_copy(k).start()
        return c

    def wait_msg(k, c):
        msg_wait(k)
        return c

    lax.fori_loop(1, n_groups, send_msg, 0)

    def decode():
        big[0].wait()
        big[1].wait()
        b = dnk.shape[0]
        q = dq[...].reshape(b, ROWS16, HEAD_DIM)
        s = lax.dot_general(
            q, ck_s[...], (((2,), (2,)), ((0,), (0,))), preferred_element_type=jnp.float32
        )
        limit = spread(context[...].astype(jnp.float32), ROWS16).reshape(b, ROWS16, 1)
        slot = lax.broadcasted_iota(jnp.int32, s.shape, 2).astype(jnp.float32)
        s = jnp.where(slot < limit, s, NEG)
        nk = dnk[...].astype(jnp.float32)
        nv = dnv[...].astype(jnp.float32)
        n0, n1 = new_scores(q.astype(jnp.float32), (nk[:, 0:1], nk[:, 1:2]))
        m = jnp.maximum(jnp.max(s, axis=2, keepdims=True), jnp.maximum(n0, n1))
        w = jnp.exp2((s - m) * RATE)
        w0 = jnp.exp2((n0 - m) * RATE)
        w1 = jnp.exp2((n1 - m) * RATE)
        total = jnp.sum(w, axis=2, keepdims=True) + w0 + w1
        o = lax.dot_general(
            w.astype(jnp.bfloat16),
            cv_s[...],
            (((2,), (1,)), ((0,), (0,))),
            preferred_element_type=jnp.float32,
        )
        o = o + w0.astype(jnp.bfloat16).astype(jnp.float32) * nv[:, 0:1]
        o = o + w1.astype(jnp.bfloat16).astype(jnp.float32) * nv[:, 1:2]
        d_out[...] = (o / total).reshape(b * ROWS16, HEAD_DIM).astype(jnp.bfloat16)

    def aq_copy(k):
        peer = (t + k) % n_tp
        return pltpu.make_async_remote_copy(
            src_ref=aq.at[t],
            dst_ref=aq.at[t],
            send_sem=q_send.at[k],
            recv_sem=q_recv.at[t],
            device_id={"tp": peer},
            device_id_type=MESH,
        )

    def aq_wait(k):
        peer = (t + k) % n_tp
        pltpu.make_async_remote_copy(
            src_ref=aq.at[peer],
            dst_ref=aq.at[peer],
            send_sem=q_send.at[k],
            recv_sem=q_recv.at[peer],
            device_id={"tp": peer},
            device_id_type=MESH,
        ).wait_recv()

    def arrivals_choose():
        own_msg.wait()
        lax.fori_loop(1, n_groups, wait_msg, 0)
        own = routes[pl.ds(g, 1), :].astype(jnp.float32)
        dest = spread(own, ROWS16)
        owner = lax.broadcasted_iota(jnp.int32, (a_rows, n_prompts), 0) // ROWS16
        other = lax.broadcasted_iota(jnp.int32, (a_rows, n_prompts), 1)
        rank = jnp.sum(
            jnp.where((dest == own) & (other < owner), 1.0, 0.0), axis=1, keepdims=True
        )
        within = lax.broadcasted_iota(jnp.int32, (a_rows, 1), 0) % ROWS16
        target = (dest * CAPACITY + rank) * ROWS16 + within.astype(jnp.float32)
        slot_rows = n_groups * CAPACITY * ROWS16
        column = lax.broadcasted_iota(jnp.int32, (a_rows, slot_rows), 1).astype(jnp.float32)
        sel[...] = jnp.where(column == target, 1.0, 0.0).astype(jnp.bfloat16)
        got = rm[:, :, 0:ROWS16, :].reshape(slot_rows, HEAD_DIM)
        aq[t] = dot_n(sel[...], got).astype(jnp.bfloat16)

        def send(k, c):
            aq_copy(k).start()
            return c

        lax.fori_loop(1, n_tp, send, 0)
        local_len = fk_s.shape[0] // n_prompts
        own_len = lengths[pl.ds(g, 1), :].astype(jnp.float32)
        limit = spread(own_len, ROWS16) - (t * local_len).astype(jnp.float32)
        col = lax.broadcasted_iota(jnp.int32, (a_rows, HEAD_DIM), 1)
        quad_row = (lax.broadcasted_iota(jnp.int32, (a_rows, HEAD_DIM), 0) // ROWS16) % 4
        keep = (col // local_len == quad_row) & ((col % local_len).astype(jnp.float32) < limit)
        bias[...] = jnp.where(keep, 0.0, NEG)

    def po_copy(h, k):
        return pltpu.make_async_remote_copy(
            src_ref=po.at[h],
            dst_ref=ro.at[t],
            send_sem=o_send.at[k],
            recv_sem=o_recv.at[t],
            device_id={"tp": h},
            device_id_type=MESH,
        )

    def ps_copy(h, k):
        return pltpu.make_async_remote_copy(
            src_ref=ps.at[h],
            dst_ref=rs.at[t],
            send_sem=s_send.at[k],
            recv_sem=s_recv.at[t],
            device_id={"tp": h},
            device_id_type=MESH,
        )

    def po_wait(k):
        peer = (t + k) % n_tp
        for send_sem, recv_sem, ref in ((o_send, o_recv, ro), (s_send, s_recv, rs)):
            pltpu.make_async_remote_copy(
                src_ref=ref.at[peer],
                dst_ref=ref.at[peer],
                send_sem=send_sem.at[k],
                recv_sem=recv_sem.at[peer],
                device_id={"tp": peer},
                device_id_type=MESH,
            ).wait_recv()

    def partial_head(h, o_ref, s_ref, at):
        cols = pl.ds(pl.multiple_of(h * HEAD_DIM, HEAD_DIM), HEAD_DIM)
        lane = lax.broadcasted_iota(jnp.int32, (4 * ROWS16, HEAD_DIM), 1)
        stats = jnp.zeros((4 * ROWS16, HEAD_DIM), jnp.float32)
        for i in range(quads):
            rows_i = slice(i * 4 * ROWS16, (i + 1) * 4 * ROWS16)
            keys_i = slice(i * HEAD_DIM, (i + 1) * HEAD_DIM)
            s = dot_t(aq[h, rows_i, :], fk_s[keys_i, cols]) + bias[rows_i, :]
            m = jnp.max(s, axis=1, keepdims=True)
            w = jnp.exp2((s - m) * RATE)
            total = jnp.sum(w, axis=1, keepdims=True)
            o_ref[at, rows_i, :] = dot_n(w.astype(jnp.bfloat16), fv_s[keys_i, cols]).astype(
                jnp.bfloat16
            )
            stats = jnp.where(lane == i, m, stats)
            stats = jnp.where(lane == quads + i, total, stats)
        s_ref[at] = stats

    def arrivals_partial():
        def wait(k, c):
            aq_wait(k)
            return c

        lax.fori_loop(1, n_tp, wait, 0)
        big[3].wait()
        big[4].wait()

        def one(k, c):
            h = (t + k) % n_tp
            partial_head(h, po, ps, h)
            po_copy(h, k).start()
            ps_copy(h, k).start()
            return c

        lax.fori_loop(1, n_tp, one, 0)
        partial_head(t, ro, rs, t)

    def ret_copy(k):
        peer = (g + k) % n_groups
        return pltpu.make_async_remote_copy(
            src_ref=ret.at[peer],
            dst_ref=ao.at[g],
            send_sem=b_send.at[k],
            recv_sem=b_recv.at[g],
            device_id={"group": peer},
            device_id_type=MESH,
        )

    def ret_wait(k):
        peer = (g + k) % n_groups
        pltpu.make_async_remote_copy(
            src_ref=ao.at[peer],
            dst_ref=ao.at[peer],
            send_sem=b_send.at[k],
            recv_sem=b_recv.at[peer],
            device_id={"group": peer},
            device_id_type=MESH,
        ).wait_recv()

    def arrivals_join():
        def wait(k, c):
            po_wait(k)
            return c

        lax.fori_loop(1, n_tp, wait, 0)
        slot_rows = n_groups * CAPACITY * ROWS16
        extra = rm[:, :, ROWS16 : 2 * ROWS16, :].reshape(slot_rows, HEAD_DIM)
        new = dot_n(sel[...], extra).reshape(n_prompts, ROWS16, HEAD_DIM)
        q3 = aq[t].astype(jnp.float32).reshape(n_prompts, ROWS16, HEAD_DIM)
        n0, n1 = new_scores(q3, (new[:, 0:1], new[:, 1:2]))
        n0 = n0.reshape(a_rows, 1)
        n1 = n1.reshape(a_rows, 1)
        ms = [
            jnp.concatenate([rs[p][:, i : i + 1] for i in range(quads)], axis=0)
            for p in range(n_tp)
        ]
        m = jnp.maximum(n0, n1)
        for mp in ms:
            m = jnp.maximum(m, mp)
        w0 = jnp.exp2((n0 - m) * RATE)
        w1 = jnp.exp2((n1 - m) * RATE)
        total = w0 + w1
        o = jnp.zeros((a_rows, HEAD_DIM), jnp.float32)
        for p in range(n_tp):
            wp = jnp.exp2((ms[p] - m) * RATE)
            lp = jnp.concatenate(
                [rs[p][:, quads + i : quads + i + 1] for i in range(quads)], axis=0
            )
            total = total + wp * lp
            o = o + wp * ro[p].astype(jnp.float32)
        w0 = w0.astype(jnp.bfloat16).astype(jnp.float32).reshape(n_prompts, ROWS16, 1)
        w1 = w1.astype(jnp.bfloat16).astype(jnp.float32).reshape(n_prompts, ROWS16, 1)
        o = o + (w0 * new[:, 2:3] + w1 * new[:, 3:4]).reshape(a_rows, HEAD_DIM)
        res = (o / total).astype(jnp.bfloat16)
        back = lax.dot_general(
            sel[...], res, (((0,), (0,)), ((), ())), preferred_element_type=jnp.float32
        )
        ret[...] = back.astype(jnp.bfloat16).reshape(n_groups, CAPACITY, ROWS16, HEAD_DIM)

        def send(k, c):
            ret_copy(k).start()
            return c

        lax.fori_loop(1, n_groups, send, 0)

    def prefill_head(h):
        vis = span_offset[0] > 0
        filled = span_offset[0] + t * rows < prompt_length[0]
        part = 4
        n_rows = part * rows
        kp = kv[h, 0].reshape(n_tp * rows, HEAD_DIM)
        ks = kv[h, 1].reshape(n_tp * rows, HEAD_DIM)
        vp = kv[h, 2].reshape(n_tp * rows, HEAD_DIM)
        vs = kv[h, 3].reshape(n_tp * rows, HEAD_DIM)
        position = lax.broadcasted_iota(jnp.int32, (n_rows, 1), 0) % rows + t * rows
        key_ids = lax.broadcasted_iota(jnp.int32, (n_rows, n_tp * rows), 1)
        live = span_offset[0] + position < prompt_length[0]

        def half(j, c):
            def cols(i):
                start = h * (GROUP_SIZE * HEAD_DIM) + (j * part + i) * HEAD_DIM
                return pl.ds(pl.multiple_of(start, HEAD_DIM), HEAD_DIM)

            q = jnp.concatenate([q_s[:, cols(i)] for i in range(part)], axis=0)
            sp = dot_t(q, kp)
            ss = jnp.where(key_ids <= position, dot_t(q, ks), NEG)
            mp = jnp.max(sp, axis=1, keepdims=True)
            m = jnp.max(ss, axis=1, keepdims=True)
            m = jnp.where(vis, jnp.maximum(m, mp), m)
            wp = jnp.exp2((sp - jnp.where(vis, m, -NEG)) * RATE)
            ws = jnp.exp2((ss - m) * RATE)
            total = jnp.sum(wp, axis=1, keepdims=True) + jnp.sum(ws, axis=1, keepdims=True)
            o = dot_n(wp.astype(jnp.bfloat16), vp) + dot_n(ws.astype(jnp.bfloat16), vs)
            o = jnp.where(live, o / total, 0.0).astype(jnp.bfloat16)
            for i in range(part):
                p_out[:, cols(i)] = o[i * rows : (i + 1) * rows]
            return c

        lax.fori_loop(0, GROUP_SIZE // part, half, 0)

    ahead = 2
    for h in range(ahead):
        stage1(h)
    decode()
    stage2(0)
    arrivals_choose()
    big[2].wait()

    def turn(s, c):
        @pl.when(s + ahead < KV_HEADS)
        def _():
            stage1(s + ahead)

        @pl.when(s + 1 < KV_HEADS)
        def _():
            stage2(s + 1)

        stage3(s)

        @pl.when(s == 1)
        def _():
            arrivals_partial()

        @pl.when(s == 4)
        def _():
            arrivals_join()

        @pl.when(s >= 1)
        def _():
            stage4(s - 1)
            prefill_head(s - 1)

        return c

    lax.fori_loop(0, KV_HEADS, turn, 0)
    stage4(KV_HEADS - 1)
    prefill_head(KV_HEADS - 1)

    def wait_ret(k, c):
        ret_wait(k)
        return c

    lax.fori_loop(1, n_groups, wait_ret, 0)
    ao[g] = ret[g]
    a_out[...] = ao[...]

    def drain_group(k, c):
        msg_copy(k).wait_send()
        ret_copy(k).wait_send()
        return c

    def drain_tp(k, c):
        h = (t + k) % n_tp
        aq_copy(k).wait_send()
        po_copy(h, k).wait_send()
        ps_copy(h, k).wait_send()
        return c

    def drain_kv(h, c):
        block_copy(h, t, 0, partner).wait_send()
        block_copy(h, t, 1, right).wait_send()
        block_copy(h, t, 2, left).wait_send()
        block_copy(h, partner, 3, right).wait_send()
        block_copy(h, partner, 4, left).wait_send()
        pair_copy(h, 0, left_x, 5, right).wait_send()
        pair_copy(h, 2, right_x, 6, left).wait_send()
        return c

    lax.fori_loop(1, n_groups, drain_group, 0)
    lax.fori_loop(1, n_tp, drain_tp, 0)
    lax.fori_loop(0, KV_HEADS, drain_kv, 0)


def to_rows(queries):
    b = queries.shape[0]
    return queries.reshape(b, STEPS, GROUP_SIZE, HEAD_DIM).transpose(0, 2, 1, 3)


def from_rows(rows, b):
    rows = rows.reshape(b, GROUP_SIZE, STEPS, HEAD_DIM).transpose(0, 2, 1, 3)
    return rows.reshape(b, STEPS, GROUP_SIZE * HEAD_DIM)


def local(
    prefill_queries,
    span_keys,
    span_values,
    prefix_keys,
    prefix_values,
    span_offsets,
    prompt_lengths,
    decode_queries,
    decode_new_keys,
    decode_new_values,
    cache_keys,
    cache_values,
    context_lengths,
    placement,
    finished_lengths,
    finished_keys,
    finished_values,
    arrival_queries,
    arrival_new_keys,
    arrival_new_values,
):
    n_groups = lax.axis_size("group")
    n_tp = lax.axis_size("tp")
    n_prompts, local_len, width = finished_keys.shape
    rows = prefill_queries.shape[0]
    dec = decode_queries.shape[0]
    slots = arrival_queries.shape[0]
    dq = to_rows(decode_queries).reshape(dec * ROWS16, HEAD_DIM)
    msg = jnp.concatenate(
        [
            to_rows(arrival_queries).reshape(slots, ROWS16, HEAD_DIM),
            arrival_new_keys,
            arrival_new_values,
            jnp.zeros((slots, ROWS16 - 2 * STEPS, HEAD_DIM), jnp.bfloat16),
        ],
        axis=1,
    ).reshape(n_groups, CAPACITY, 2 * ROWS16, HEAD_DIM)
    any_ = pl.BlockSpec(memory_space=pl.ANY)
    vmem = pl.BlockSpec(memory_space=pltpu.VMEM)
    smem = pl.BlockSpec(memory_space=pltpu.SMEM)
    bf, f32 = jnp.bfloat16, jnp.float32
    a_rows = n_prompts * ROWS16
    dma = pltpu.SemaphoreType.DMA
    p_out, d_out, a_out = pl.pallas_call(
        functools.partial(body, n_groups, n_tp),
        out_shape=(
            jax.ShapeDtypeStruct(prefill_queries.shape, bf),
            jax.ShapeDtypeStruct(dq.shape, bf),
            jax.ShapeDtypeStruct((n_groups, CAPACITY, ROWS16, HEAD_DIM), bf),
        ),
        in_specs=[any_] * 5
        + [smem] * 2
        + [vmem] * 3
        + [any_] * 2
        + [vmem] * 3
        + [any_] * 2
        + [any_],
        out_specs=[vmem] * 3,
        scratch_shapes=[
            pltpu.VMEM((KV_HEADS, 4, n_tp, rows, HEAD_DIM), bf),
            pltpu.VMEM(prefill_queries.shape, bf),
            pltpu.VMEM(cache_keys.shape, bf),
            pltpu.VMEM(cache_values.shape, bf),
            pltpu.VMEM((n_prompts * local_len, width), bf),
            pltpu.VMEM((n_prompts * local_len, width), bf),
            pltpu.VMEM(msg.shape, bf),
            pltpu.VMEM((n_tp, a_rows, HEAD_DIM), bf),
            pltpu.VMEM((n_tp, a_rows, HEAD_DIM), bf),
            pltpu.VMEM((n_tp, a_rows, HEAD_DIM), bf),
            pltpu.VMEM((n_tp, 4 * ROWS16, HEAD_DIM), f32),
            pltpu.VMEM((n_tp, 4 * ROWS16, HEAD_DIM), f32),
            pltpu.VMEM((a_rows, slots * ROWS16), bf),
            pltpu.VMEM((a_rows, HEAD_DIM), f32),
            pltpu.VMEM((n_groups, CAPACITY, ROWS16, HEAD_DIM), bf),
            pltpu.VMEM((n_groups, CAPACITY, ROWS16, HEAD_DIM), bf),
            dma((KV_HEADS, 4)),
            dma((5,)),
            dma((KV_HEADS, 7)),
            dma((KV_HEADS, 7)),
            dma((n_groups,)),
            dma((n_groups,)),
            dma((n_tp,)),
            dma((n_tp,)),
            dma((n_tp,)),
            dma((n_tp,)),
            dma((n_tp,)),
            dma((n_tp,)),
            dma((n_groups,)),
            dma((n_groups,)),
            dma(()),
        ],
        compiler_params=pltpu.CompilerParams(
            collective_id=0, has_side_effects=True, vmem_limit_bytes=56 * 1024 * 1024
        ),
    )(
        prefill_queries,
        span_keys,
        span_values,
        prefix_keys,
        prefix_values,
        span_offsets,
        prompt_lengths,
        dq,
        decode_new_keys,
        decode_new_values,
        cache_keys,
        cache_values,
        context_lengths[None, :],
        placement.reshape(n_groups, n_prompts),
        finished_lengths.reshape(n_groups, n_prompts),
        finished_keys.reshape(n_prompts * local_len, width),
        finished_values.reshape(n_prompts * local_len, width),
        msg,
    )
    return (p_out, from_rows(d_out, dec), from_rows(a_out, slots))


def solution(mesh):
    both = P(("group", "tp"), None)
    heads = P("group", None, "tp")
    placed = (
        (both,) * 5
        + (P("group"),) * 2
        + (heads,) * 5
        + (P("group"), P(), P())
        + (P("group", "tp", None),) * 2
        + (heads,) * 3
    )
    return jax.shard_map(
        local,
        mesh=mesh,
        in_specs=placed,
        out_specs=(both, heads, heads),
        check_vma=False,
    )
```

time: 547 us -> 145 us (0.27)
  the two profiles are of different devices: /device:TPU:32 before, /device:TPU:8 now
where the time goes in v1:
time: 145 us; the launch traced here: 142 us
  Pallas kernels  131 us (90%)
  local copies, waits for them, and re-layouts  7.31 us (5%)
  other arithmetic  2.03 us (1%)
  between operations  1.96 us (1%)
    pallas_call x1, Pallas kernels, local(): pl.pallas_call(functools.partial(body, n_groups, n_tp), out_shape=(jax.Sh...  131 us
    unnamed x7, local copies, waits for them, and re-layouts  4.51 us

profile of v1, /device:TPU:8, one launch (start us, length us, event | category | flops | bytes accessed | tf_op | source)
XLA Modules:
  0.0 142.2 jit_solution(8571074329484296003)
XLA Ops:
  1.9 0.1 pad.3.clone
  2.0 1.4 reshape.48.routes
  3.4 1.4 reshape.49.lengths
  4.7 2.0 %maximum_maximum_fusion.msg = bf16[32,2,32,128]{3,2,1,0:T(8,128)(2,1)} fusion(bf16[32,2,2,128]{3,2,1,0:T(2,128)(2,1)} %bitcast.31, bf16[32,2,2,128]{3,2,1,0:T(2,128)(2,1)} %bitcast.32, bf16[32,2,16,128]{3,2,1,0:T(8,128)(2,1)} %bitcast.27, bf16[32]{0:T(256)(128)(2,1)S(1)} %pad.3.clone), kind=kLoop, calls=%fused_computation | loop fusion | flops 2097152 | bytes 852032 | tf_op jit(solution)/shard_map/concatenate | solution.py:595
  6.8 130.9 %shard_map.211 = (bf16[128,8192]{1,0:T(8,128)(2,1)}, bf16[512,128]{1,0:T(8,128)(2,1)}, bf16[32,2,16,128]{3,2,1,0:T(8,128)(2,1)}) custom-call(bf16[128,8192]{1,0:T(8,128)(2,1)} %pq.1, bf16[128,1024]{1,0:T(8,128)(2,1)} %sk.1, bf16[128,1024]{1,0:T(8,128)(2,1)} %sv.1, bf16[128,1024]{1,0:T(8,128)(2,1)} %pk.1, bf16[128,1024]{1,0:T(8,128)(2,1)} %pv.1, ...), custom_call_target="tpu_custom_call" | custom-call | tf_op jit(solution)/shard_map/pallas_call | solution.py:610
  137.7 0.0 copy-start.1
  137.7 0.0 copy-start
  137.7 3.1 %copy.32 = bf16[128,8192]{1,0:T(8,128)(2,1)} copy(bf16[128,8192]{1,0:T(8,128)(2,1)} %get-tuple-element.12) | data formatting | bytes 4194304
  140.9 0.0 copy-done.1
  140.9 0.7 copy.33
  141.5 0.0 copy-done
  141.5 0.7 copy.34
  (1 shorter events, 0.0 us)
Async XLA Ops:
  137.7 3.2 %copy-start.1 = (bf16[512,128]{1,0:T(8,128)(2,1)S(1)}, bf16[512,128]{1,0:T(8,128)(2,1)}, u32[]{:S(2)}) copy-start(bf16[512,128]{1,0:T(8,128)(2,1)} %get-tuple-element.7) | copy-start | bytes 393220
  137.7 3.8 %copy-start = (bf16[32,2,16,128]{3,2,1,0:T(8,128)(2,1)S(1)}, bf16[32,2,16,128]{3,2,1,0:T(8,128)(2,1)}, u32[]{:S(2)}) copy-start(bf16[32,2,16,128]{3,2,1,0:T(8,128)(2,1)} %get-tuple-element.8) | copy-start | bytes 786436

commit v2 on v1

--- a/solution.py
+++ b/solution.py
@@ -18,6 +18,9 @@
 NEG = -1e30
 RATE = math.log2(math.e) / math.sqrt(HEAD_DIM)
 X_CHIPS = 4
+CORES = 2
+ITEMS = KV_HEADS + 1
+QUERY_ITEM = KV_HEADS
 
 
 def dot_t(a, b):
@@ -28,10 +31,10 @@
     return lax.dot_general(a, b, (((1,), (0,)), ((), ())), preferred_element_type=jnp.float32)
 
 
-def spread(row, reps):
-    n = row.shape[1]
-    owner = lax.broadcasted_iota(jnp.int32, (n * reps, n), 0) // reps
-    lane = lax.broadcasted_iota(jnp.int32, (n * reps, n), 1)
+def spread(row, count, reps, base):
+    shape = (count * reps, row.shape[1])
+    owner = lax.broadcasted_iota(jnp.int32, shape, 0) // reps + base
+    lane = lax.broadcasted_iota(jnp.int32, shape, 1)
     return jnp.sum(jnp.where(owner == lane, row, 0.0), axis=1, keepdims=True)
 
 
@@ -63,7 +66,9 @@
     lengths,
     fk,
     fv,
-    msg,
+    arrival_q,
+    ank,
+    anv,
     p_out,
     d_out,
     a_out,
@@ -73,8 +78,9 @@
     cv_s,
     fk_s,
     fv_s,
+    rel,
+    msg,
     rm,
-    aq,
     po,
     ro,
     ps,
@@ -89,15 +95,13 @@
     x_recv,
     m_send,
     m_recv,
-    q_send,
-    q_recv,
     o_send,
     o_recv,
     s_send,
     s_recv,
     b_send,
     b_recv,
-    own_sem,
+    out_sem,
 ):
     g = lax.axis_index("group")
     t = lax.axis_index("tp")
@@ -108,7 +112,10 @@
     right_x = (x + 1) % X_CHIPS
     left_x = (x + X_CHIPS - 1) % X_CHIPS
     far_x = (x + 2) % X_CHIPS
-    n_prompts = routes.shape[1]
+    yl = (g // CORES) % 2
+    beside = g + CORES * (1 - 2 * yl)
+    local_len = HEAD_DIM // 4
+    n_prompts = fk_s.shape[0] // local_len
     a_rows = n_prompts * ROWS16
     quads = n_prompts // 4
     rows = pq.shape[0]
@@ -117,7 +124,7 @@
 
     def kv_load(h, a):
         cols = pl.ds(pl.multiple_of(h * HEAD_DIM, HEAD_DIM), HEAD_DIM)
-        return pltpu.make_async_copy(arrays[a].at[:, cols], kv.at[h, a, t], load_kv.at[h, a])
+        return pltpu.make_async_copy(arrays[a].at[:, cols], kv.at[h, a, x, yh], load_kv.at[h, a])
 
     def start_loads(h, c):
         for a in range(4):
@@ -133,8 +140,6 @@
     ]
     for copy in big:
         copy.start()
-    own_msg = pltpu.make_async_copy(msg.at[g], rm.at[g], own_sem)
-    own_msg.start()
 
     barrier = pltpu.get_barrier_semaphore()
 
@@ -150,49 +155,181 @@
 
     lax.fori_loop(1, n_groups, greet_group, 0)
     lax.fori_loop(1, n_tp, greet_tp, 0)
-    pl.semaphore_wait(barrier, n_groups - 1 + n_tp - 1)
-
-    def to_tp(src, dst, kind, h, peer):
+    pl.semaphore_signal(
+        barrier, inc=1, device_id={"group": beside, "tp": partner}, device_id_type=MESH
+    )
+    pl.semaphore_wait(barrier, n_groups - 1 + n_tp - 1 + 1)
+
+    to_right, to_left = {"tp": right}, {"tp": left}
+    to_same, to_cross = {"group": beside}, {"group": beside, "tp": partner}
+    ny = 1 - yh
+
+    def y_first(i):
+        return i % 3 != 1
+
+    def hop(src, dst, kind, i, device):
         return pltpu.make_async_remote_copy(
             src_ref=src,
             dst_ref=dst,
-            send_sem=x_send.at[h, kind],
-            recv_sem=x_recv.at[h, kind],
-            device_id={"tp": peer},
+            send_sem=x_send.at[i, kind],
+            recv_sem=x_recv.at[i, kind],
+            device_id=device,
             device_id_type=MESH,
         )
 
-    def block_copy(h, block, kind, peer):
-        ref = kv.at[h, :, block]
-        return to_tp(ref, ref, kind, h, peer)
-
-    def pair_copy(h, arr, xs, kind, peer):
-        ref = kv.at[h, pl.ds(arr, 2), pl.ds(xs * 2, 2)]
-        return to_tp(ref, ref, kind, h, peer)
-
-    def stage1(h):
+    def same(ref, kind, i, device):
+        return hop(ref, ref, kind, i, device)
+
+    keys, values = pl.ds(0, 2), pl.ds(2, 2)
+
+    def own_right(i, xs):
+        return same(kv.at[i, :, xs, yh], 0, i, to_right)
+
+    def own_left(i, xs):
+        return same(kv.at[i, :, xs, yh], 1, i, to_left)
+
+    def one_y(i, part):
+        rows_of = keys if part == 0 else values
+        device = to_same if part == 0 else to_cross
+        return hop(kv.at[i, rows_of, x, yh], rel.at[i, part, :, 0], 2 + part, i, device)
+
+    def all_y(i, part):
+        rows_of = keys if part == 0 else values
+        device = to_same if part == 0 else to_cross
+        return hop(kv.at[i, rows_of, :, yh], rel.at[i, part], 2 + part, i, device)
+
+    def one_relay(i, part):
+        if part == 0:
+            return hop(rel.at[i, 0, :, 0], kv.at[i, keys, x, yh], 4, i, to_cross)
+        return hop(rel.at[i, 1, :, 0], kv.at[i, values, x, ny], 5, i, to_same)
+
+    def all_relay(i, part):
+        if part == 0:
+            return hop(rel.at[i, 0], kv.at[i, keys, :, yh], 4, i, to_cross)
+        return hop(rel.at[i, 1], kv.at[i, values, :, ny], 5, i, to_same)
+
+    def one_landed(i, part):
+        return same(kv.at[i, (keys, values)[part], x, ny], 4 + part, i, to_same)
+
+    def all_landed(i, part):
+        return same(kv.at[i, (keys, values)[part], :, ny], 4 + part, i, to_same)
+
+    def partner_right(i, xs):
+        return same(kv.at[i, :, xs, ny], 6, i, to_right)
+
+    def partner_left(i, xs):
+        return same(kv.at[i, :, xs, ny], 7, i, to_left)
+
+    def pair_right(i, xs):
+        return same(kv.at[i, keys, xs], 8, i, to_right)
+
+    def pair_left(i, xs):
+        return same(kv.at[i, values, xs], 9, i, to_left)
+
+    def single_right(i, xs):
+        return same(kv.at[i, keys, xs, yh], 8, i, to_right)
+
+    def single_left(i, xs):
+        return same(kv.at[i, values, xs, yh], 9, i, to_left)
+
+    def by_kind(i, first, second):
+        pl.when(y_first(i))(lambda: first(i))
+        pl.when(jnp.logical_not(y_first(i)))(lambda: second(i))
+
+    def stage1(i):
+        @pl.when(y_first(i))
+        def _():
+            one_y(i, 0).start()
+            one_y(i, 1).start()
+
+        own_right(i, x).start()
+        own_left(i, x).start()
+
+    def first_a(i):
+        for part in range(2):
+            one_y(i, part).wait_recv()
+            one_relay(i, part).start()
+
+    def first_b(i):
+        one_landed(i, 0).wait_recv()
+        one_landed(i, 1).wait_recv()
+        partner_right(i, x).start()
+        partner_left(i, x).start()
+
+    def first_c(i):
+        own_right(i, left_x).wait_recv()
+        partner_right(i, left_x).wait_recv()
+        pair_right(i, left_x).start()
+        own_left(i, right_x).wait_recv()
+        partner_left(i, right_x).wait_recv()
+        pair_left(i, right_x).start()
+
+    def first_d(i):
+        pair_right(i, far_x).wait_recv()
+        pair_left(i, far_x).wait_recv()
+
+    def second_a(i):
+        own_right(i, left_x).wait_recv()
+        single_right(i, left_x).start()
+        own_left(i, right_x).wait_recv()
+        single_left(i, right_x).start()
+
+    def second_b(i):
+        single_right(i, far_x).wait_recv()
+        single_left(i, far_x).wait_recv()
+        all_y(i, 0).start()
+        all_y(i, 1).start()
+
+    def second_c(i):
+        for part in range(2):
+            all_y(i, part).wait_recv()
+            all_relay(i, part).start()
+
+    def second_d(i):
+        all_landed(i, 0).wait_recv()
+        all_landed(i, 1).wait_recv()
+
+    def stage_a(i):
+        by_kind(i, first_a, second_a)
+
+    def stage_b(i):
+        by_kind(i, first_b, second_b)
+
+    def stage_c(i):
+        by_kind(i, first_c, second_c)
+
+    def stage_d(i):
+        by_kind(i, first_d, second_d)
+
+    def first_drain(i):
+        for part in range(2):
+            one_y(i, part).wait_send()
+            one_relay(i, part).wait_send()
+        partner_right(i, x).wait_send()
+        partner_left(i, x).wait_send()
+        pair_right(i, left_x).wait_send()
+        pair_left(i, right_x).wait_send()
+
+    def second_drain(i):
+        for part in range(2):
+            all_y(i, part).wait_send()
+            all_relay(i, part).wait_send()
+        single_right(i, left_x).wait_send()
+        single_left(i, right_x).wait_send()
+
+    def drain_item(i, c):
+        own_right(i, x).wait_send()
+        own_left(i, x).wait_send()
+        by_kind(i, first_drain, second_drain)
+        return c
+
+    def start_item(i, c):
         for a in range(4):
-            kv_load(h, a).wait()
-        block_copy(h, t, 0, partner).start()
-        block_copy(h, t, 1, right).start()
-        block_copy(h, t, 2, left).start()
-
-    def stage2(h):
-        block_copy(h, partner, 0, partner).wait_recv()
-        block_copy(h, partner, 3, right).start()
-        block_copy(h, partner, 4, left).start()
-
-    def stage3(h):
-        block_copy(h, left_x * 2 + yh, 1, right).wait_recv()
-        block_copy(h, left_x * 2 + (1 - yh), 3, right).wait_recv()
-        pair_copy(h, 0, left_x, 5, right).start()
-        block_copy(h, right_x * 2 + yh, 2, left).wait_recv()
-        block_copy(h, right_x * 2 + (1 - yh), 4, left).wait_recv()
-        pair_copy(h, 2, right_x, 6, left).start()
-
-    def stage4(h):
-        pair_copy(h, 0, far_x, 5, right).wait_recv()
-        pair_copy(h, 2, far_x, 6, left).wait_recv()
+            kv_load(i, a).wait()
+        stage1(i)
+        return c
+
+    lax.fori_loop(0, KV_HEADS, start_item, 0)
 
     def msg_copy(k):
         peer = (g + k) % n_groups
@@ -224,7 +361,17 @@
         msg_wait(k)
         return c
 
+    pair = (n_groups, CAPACITY, ROWS16, HEAD_DIM)
+    row_id = lax.broadcasted_iota(jnp.int32, (1, ROWS16, 1), 1)
+    extra = jnp.zeros((n_groups * CAPACITY, ROWS16, HEAD_DIM), jnp.float32)
+    for step in range(STEPS):
+        nk = ank[...].astype(jnp.float32)[:, step : step + 1]
+        nv = anv[...].astype(jnp.float32)[:, step : step + 1]
+        extra = jnp.where(row_id == step, nk, jnp.where(row_id == STEPS + step, nv, extra))
+    msg[:, :, 0:ROWS16, :] = arrival_q[...]
+    msg[:, :, ROWS16 : 2 * ROWS16, :] = extra.astype(jnp.bfloat16).reshape(pair)
     lax.fori_loop(1, n_groups, send_msg, 0)
+    rm[g] = msg[g]
 
     def decode():
         big[0].wait()
@@ -234,7 +381,7 @@
         s = lax.dot_general(
             q, ck_s[...], (((2,), (2,)), ((0,), (0,))), preferred_element_type=jnp.float32
         )
-        limit = spread(context[...].astype(jnp.float32), ROWS16).reshape(b, ROWS16, 1)
+        limit = spread(context[...].astype(jnp.float32), b, ROWS16, 0).reshape(b, ROWS16, 1)
         slot = lax.broadcasted_iota(jnp.int32, s.shape, 2).astype(jnp.float32)
         s = jnp.where(slot < limit, s, NEG)
         nk = dnk[...].astype(jnp.float32)
@@ -255,37 +402,30 @@
         o = o + w1.astype(jnp.bfloat16).astype(jnp.float32) * nv[:, 1:2]
         d_out[...] = (o / total).reshape(b * ROWS16, HEAD_DIM).astype(jnp.bfloat16)
 
-    def aq_copy(k):
-        peer = (t + k) % n_tp
-        return pltpu.make_async_remote_copy(
-            src_ref=aq.at[t],
-            dst_ref=aq.at[t],
-            send_sem=q_send.at[k],
-            recv_sem=q_recv.at[t],
-            device_id={"tp": peer},
-            device_id_type=MESH,
-        )
-
-    def aq_wait(k):
-        peer = (t + k) % n_tp
-        pltpu.make_async_remote_copy(
-            src_ref=aq.at[peer],
-            dst_ref=aq.at[peer],
-            send_sem=q_send.at[k],
-            recv_sem=q_recv.at[peer],
-            device_id={"tp": peer},
-            device_id_type=MESH,
-        ).wait_recv()
+    def quad_rows(i):
+        half = i % 2 * (4 * ROWS16)
+        return i // 2, slice(half, half + 4 * ROWS16)
+
+    def queries_of(xs, ys):
+        parts = []
+        for i in range(quads):
+            block, part = quad_rows(i)
+            parts.append(kv[QUERY_ITEM, block, xs, ys, part, :])
+        return jnp.concatenate(parts, axis=0)
 
     def arrivals_choose():
-        own_msg.wait()
         lax.fori_loop(1, n_groups, wait_msg, 0)
-        own = routes[pl.ds(g, 1), :].astype(jnp.float32)
-        dest = spread(own, ROWS16)
-        owner = lax.broadcasted_iota(jnp.int32, (a_rows, n_prompts), 0) // ROWS16
-        other = lax.broadcasted_iota(jnp.int32, (a_rows, n_prompts), 1)
+        lanes = routes.shape[1]
+        per_row = lanes // n_prompts
+        base = g % per_row * n_prompts
+        own = routes[pl.ds(g // per_row, 1), :].astype(jnp.float32)
+        dest = spread(own, n_prompts, ROWS16, base)
+        owner = lax.broadcasted_iota(jnp.int32, (a_rows, lanes), 0) // ROWS16
+        other = lax.broadcasted_iota(jnp.int32, (a_rows, lanes), 1) - base
         rank = jnp.sum(
-            jnp.where((dest == own) & (other < owner), 1.0, 0.0), axis=1, keepdims=True
+            jnp.where((dest == own) & (other >= 0) & (other < owner), 1.0, 0.0),
+            axis=1,
+            keepdims=True,
         )
         within = lax.broadcasted_iota(jnp.int32, (a_rows, 1), 0) % ROWS16
         target = (dest * CAPACITY + rank) * ROWS16 + within.astype(jnp.float32)
@@ -293,16 +433,13 @@
         column = lax.broadcasted_iota(jnp.int32, (a_rows, slot_rows), 1).astype(jnp.float32)
         sel[...] = jnp.where(column == target, 1.0, 0.0).astype(jnp.bfloat16)
         got = rm[:, :, 0:ROWS16, :].reshape(slot_rows, HEAD_DIM)
-        aq[t] = dot_n(sel[...], got).astype(jnp.bfloat16)
-
-        def send(k, c):
-            aq_copy(k).start()
-            return c
-
-        lax.fori_loop(1, n_tp, send, 0)
-        local_len = fk_s.shape[0] // n_prompts
-        own_len = lengths[pl.ds(g, 1), :].astype(jnp.float32)
-        limit = spread(own_len, ROWS16) - (t * local_len).astype(jnp.float32)
+        chosen = dot_n(sel[...], got).astype(jnp.bfloat16)
+        for i in range(quads):
+            block, part = quad_rows(i)
+            kv[QUERY_ITEM, block, x, yh, part, :] = chosen[i * 4 * ROWS16 : (i + 1) * 4 * ROWS16]
+        stage1(QUERY_ITEM)
+        own_len = lengths[pl.ds(g // per_row, 1), :].astype(jnp.float32)
+        limit = spread(own_len, n_prompts, ROWS16, base) - (t * local_len).astype(jnp.float32)
         col = lax.broadcasted_iota(jnp.int32, (a_rows, HEAD_DIM), 1)
         quad_row = (lax.broadcasted_iota(jnp.int32, (a_rows, HEAD_DIM), 0) // ROWS16) % 4
         keep = (col // local_len == quad_row) & ((col % local_len).astype(jnp.float32) < limit)
@@ -347,7 +484,9 @@
         for i in range(quads):
             rows_i = slice(i * 4 * ROWS16, (i + 1) * 4 * ROWS16)
             keys_i = slice(i * HEAD_DIM, (i + 1) * HEAD_DIM)
-            s = dot_t(aq[h, rows_i, :], fk_s[keys_i, cols]) + bias[rows_i, :]
+            block, part = quad_rows(i)
+            q = kv[QUERY_ITEM, block, h // 2, h % 2, part, :]
+            s = dot_t(q, fk_s[keys_i, cols]) + bias[rows_i, :]
             m = jnp.max(s, axis=1, keepdims=True)
             w = jnp.exp2((s - m) * RATE)
             total = jnp.sum(w, axis=1, keepdims=True)
@@ -359,11 +498,7 @@
         s_ref[at] = stats
 
     def arrivals_partial():
-        def wait(k, c):
-            aq_wait(k)
-            return c
-
-        lax.fori_loop(1, n_tp, wait, 0)
+        stage_d(QUERY_ITEM)
         big[3].wait()
         big[4].wait()
 
@@ -408,7 +543,7 @@
         slot_rows = n_groups * CAPACITY * ROWS16
         extra = rm[:, :, ROWS16 : 2 * ROWS16, :].reshape(slot_rows, HEAD_DIM)
         new = dot_n(sel[...], extra).reshape(n_prompts, ROWS16, HEAD_DIM)
-        q3 = aq[t].astype(jnp.float32).reshape(n_prompts, ROWS16, HEAD_DIM)
+        q3 = queries_of(x, yh).astype(jnp.float32).reshape(n_prompts, ROWS16, HEAD_DIM)
         n0, n1 = new_scores(q3, (new[:, 0:1], new[:, 1:2]))
         n0 = n0.reshape(a_rows, 1)
         n1 = n1.reshape(a_rows, 1)
@@ -447,7 +582,6 @@
 
     def prefill_head(h):
         vis = span_offset[0] > 0
-        filled = span_offset[0] + t * rows < prompt_length[0]
         part = 4
         n_rows = part * rows
         kp = kv[h, 0].reshape(n_tp * rows, HEAD_DIM)
@@ -475,48 +609,61 @@
             o = dot_n(wp.astype(jnp.bfloat16), vp) + dot_n(ws.astype(jnp.bfloat16), vs)
             o = jnp.where(live, o / total, 0.0).astype(jnp.bfloat16)
             for i in range(part):
-                p_out[:, cols(i)] = o[i * rows : (i + 1) * rows]
+                q_s[:, cols(i)] = o[i * rows : (i + 1) * rows]
             return c
 
         lax.fori_loop(0, GROUP_SIZE // part, half, 0)
 
-    ahead = 2
-    for h in range(ahead):
-        stage1(h)
+    def head_out(h):
+        width = GROUP_SIZE * HEAD_DIM
+        cols = pl.ds(pl.multiple_of(h * width, width), width)
+        return pltpu.make_async_copy(q_s.at[:, cols], p_out.at[:, cols], out_sem.at[h])
+
     decode()
-    stage2(0)
+    for h in range(3):
+        stage_a(h)
     arrivals_choose()
+    for h in range(2):
+        stage_b(h)
+    stage_c(0)
+    stage_a(QUERY_ITEM)
     big[2].wait()
 
     def turn(s, c):
-        @pl.when(s + ahead < KV_HEADS)
+        @pl.when(s + 3 < KV_HEADS)
         def _():
-            stage1(s + ahead)
+            stage_a(s + 3)
+
+        @pl.when(s + 2 < KV_HEADS)
+        def _():
+            stage_b(s + 2)
 
         @pl.when(s + 1 < KV_HEADS)
         def _():
-            stage2(s + 1)
-
-        stage3(s)
+            stage_c(s + 1)
+
+        @pl.when(s == 0)
+        def _():
+            stage_b(QUERY_ITEM)
 
         @pl.when(s == 1)
         def _():
+            stage_c(QUERY_ITEM)
+
+        @pl.when(s == 2)
+        def _():
             arrivals_partial()
 
-        @pl.when(s == 4)
+        @pl.when(s == 5)
         def _():
             arrivals_join()
 
-        @pl.when(s >= 1)
-        def _():
-            stage4(s - 1)
-            prefill_head(s - 1)
-
+        stage_d(s)
+        prefill_head(s)
+        head_out(s).start()
         return c
 
     lax.fori_loop(0, KV_HEADS, turn, 0)
-    stage4(KV_HEADS - 1)
-    prefill_head(KV_HEADS - 1)
 
     def wait_ret(k, c):
         ret_wait(k)
@@ -533,24 +680,18 @@
 
     def drain_tp(k, c):
         h = (t + k) % n_tp
-        aq_copy(k).wait_send()
         po_copy(h, k).wait_send()
         ps_copy(h, k).wait_send()
         return c
 
-    def drain_kv(h, c):
-        block_copy(h, t, 0, partner).wait_send()
-        block_copy(h, t, 1, right).wait_send()
-        block_copy(h, t, 2, left).wait_send()
-        block_copy(h, partner, 3, right).wait_send()
-        block_copy(h, partner, 4, left).wait_send()
-        pair_copy(h, 0, left_x, 5, right).wait_send()
-        pair_copy(h, 2, right_x, 6, left).wait_send()
+    def drain_out(h, c):
+        head_out(h).wait()
         return c
 
     lax.fori_loop(1, n_groups, drain_group, 0)
     lax.fori_loop(1, n_tp, drain_tp, 0)
-    lax.fori_loop(0, KV_HEADS, drain_kv, 0)
+    lax.fori_loop(0, ITEMS, drain_item, 0)
+    lax.fori_loop(0, KV_HEADS, drain_out, 0)
 
 
 def to_rows(queries):
@@ -592,15 +733,8 @@
     dec = decode_queries.shape[0]
     slots = arrival_queries.shape[0]
     dq = to_rows(decode_queries).reshape(dec * ROWS16, HEAD_DIM)
-    msg = jnp.concatenate(
-        [
-            to_rows(arrival_queries).reshape(slots, ROWS16, HEAD_DIM),
-            arrival_new_keys,
-            arrival_new_values,
-            jnp.zeros((slots, ROWS16 - 2 * STEPS, HEAD_DIM), jnp.bfloat16),
-        ],
-        axis=1,
-    ).reshape(n_groups, CAPACITY, 2 * ROWS16, HEAD_DIM)
+    arrival_rows = to_rows(arrival_queries).reshape(n_groups, CAPACITY, ROWS16, HEAD_DIM)
+    lanes = min(128, placement.shape[0])
     any_ = pl.BlockSpec(memory_space=pl.ANY)
     vmem = pl.BlockSpec(memory_space=pltpu.VMEM)
     smem = pl.BlockSpec(memory_space=pltpu.SMEM)
@@ -620,17 +754,18 @@
         + [any_] * 2
         + [vmem] * 3
         + [any_] * 2
-        + [any_],
-        out_specs=[vmem] * 3,
+        + [vmem] * 3,
+        out_specs=[any_, vmem, vmem],
         scratch_shapes=[
-            pltpu.VMEM((KV_HEADS, 4, n_tp, rows, HEAD_DIM), bf),
+            pltpu.VMEM((ITEMS, 4, X_CHIPS, 2, rows, HEAD_DIM), bf),
             pltpu.VMEM(prefill_queries.shape, bf),
             pltpu.VMEM(cache_keys.shape, bf),
             pltpu.VMEM(cache_values.shape, bf),
             pltpu.VMEM((n_prompts * local_len, width), bf),
             pltpu.VMEM((n_prompts * local_len, width), bf),
-            pltpu.VMEM(msg.shape, bf),
-            pltpu.VMEM((n_tp, a_rows, HEAD_DIM), bf),
+            pltpu.VMEM((ITEMS, 2, 2, X_CHIPS, rows, HEAD_DIM), bf),
+            pltpu.VMEM((n_groups, CAPACITY, 2 * ROWS16, HEAD_DIM), bf),
+            pltpu.VMEM((n_groups, CAPACITY, 2 * ROWS16, HEAD_DIM), bf),
             pltpu.VMEM((n_tp, a_rows, HEAD_DIM), bf),
             pltpu.VMEM((n_tp, a_rows, HEAD_DIM), bf),
             pltpu.VMEM((n_tp, 4 * ROWS16, HEAD_DIM), f32),
@@ -641,19 +776,17 @@
             pltpu.VMEM((n_groups, CAPACITY, ROWS16, HEAD_DIM), bf),
             dma((KV_HEADS, 4)),
             dma((5,)),
-            dma((KV_HEADS, 7)),
-            dma((KV_HEADS, 7)),
+            dma((ITEMS, 10)),
+            dma((ITEMS, 10)),
             dma((n_groups,)),
             dma((n_groups,)),
             dma((n_tp,)),
             dma((n_tp,)),
             dma((n_tp,)),
             dma((n_tp,)),
-            dma((n_tp,)),
-            dma((n_tp,)),
             dma((n_groups,)),
             dma((n_groups,)),
-            dma(()),
+            dma((KV_HEADS,)),
         ],
         compiler_params=pltpu.CompilerParams(
             collective_id=0, has_side_effects=True, vmem_limit_bytes=56 * 1024 * 1024
@@ -672,11 +805,13 @@
         cache_keys,
         cache_values,
         context_lengths[None, :],
-        placement.reshape(n_groups, n_prompts),
-        finished_lengths.reshape(n_groups, n_prompts),
+        placement.reshape(-1, lanes),
+        finished_lengths.reshape(-1, lanes),
         finished_keys.reshape(n_prompts * local_len, width),
         finished_values.reshape(n_prompts * local_len, width),
-        msg,
+        arrival_rows,
+        arrival_new_keys,
+        arrival_new_values,
     )
     return (p_out, from_rows(d_out, dec), from_rows(a_out, slots))
 

time: 145 us -> 135 us (0.931); the launches traced: 142 us -> 134 us
  Pallas kernels: 131 us -> 128 us
  local copies, waits for them, and re-layouts: 7.31 us -> 4.51 us
  other arithmetic: 2.03 us -> 0 us
    pallas_call x1, Pallas kernels: 131 us -> 128 us  [local(): pl.pallas_call(functools.partial(body, n_groups, n_tp), out_shape=(jax.Sh...]
    reshape x2 -> x0, local copies, waits for them, and re-layouts: 2.72 us -> none  [the longest x1 1.36 us: local(): placement.reshape(n_groups, n_prompts)]
    concatenate x1 -> x0, other arithmetic: 2.03 us -> none  [local(): jnp.concatenate([to_rows(arrival_queries).reshape(slots, ROWS16, HEAD_DIM...]
where the time goes in v2:
time: 135 us; the launch traced here: 134 us
  Pallas kernels  128 us (95%)
  local copies, waits for them, and re-layouts  4.51 us (3%)
  between operations  1.95 us (1%)
    pallas_call x1, Pallas kernels, local(): pl.pallas_call(functools.partial(body, n_groups, n_tp), out_shape=(jax.Sh...  128 us
    unnamed x7, local copies, waits for them, and re-layouts  4.51 us

profile of v2, /device:TPU:8, one launch (start us, length us, event | category | flops | bytes accessed | tf_op | source)
XLA Modules:
  0.0 134.5 jit_solution(468529398437713351)
XLA Ops:
  1.9 128.0 %shard_map.211 = (bf16[128,8192]{1,0:T(8,128)(2,1)}, bf16[512,128]{1,0:T(8,128)(2,1)}, bf16[32,2,16,128]{3,2,1,0:T(8,128)(2,1)}) custom-call(bf16[128,8192]{1,0:T(8,128)(2,1)} %pq.1, bf16[128,1024]{1,0:T(8,128)(2,1)} %sk.1, bf16[128,1024]{1,0:T(8,128)(2,1)} %sv.1, bf16[128,1024]{1,0:T(8,128)(2,1)} %pk.1, bf16[128,1024]{1,0:T(8,128)(2,1)} %pv.1, ...), custom_call_target="tpu_custom_call" | custom-call | tf_op jit(solution)/shard_map/pallas_call | solution.py:744
  130.0 0.0 copy-start.1
  130.0 0.0 copy-start
  130.0 3.1 %copy.32 = bf16[128,8192]{1,0:T(8,128)(2,1)} copy(bf16[128,8192]{1,0:T(8,128)(2,1)} %get-tuple-element.12) | data formatting | bytes 4194304
  133.1 0.0 copy-done.1
  133.1 0.7 copy.33
  133.8 0.0 copy-done
  133.8 0.7 copy.34
Async XLA Ops:
  130.0 3.2 %copy-start.1 = (bf16[512,128]{1,0:T(8,128)(2,1)S(1)}, bf16[512,128]{1,0:T(8,128)(2,1)}, u32[]{:S(2)}) copy-start(bf16[512,128]{1,0:T(8,128)(2,1)} %get-tuple-element.7) | copy-start | bytes 393220
  130.0 3.8 %copy-start = (bf16[32,2,16,128]{3,2,1,0:T(8,128)(2,1)S(1)}, bf16[32,2,16,128]{3,2,1,0:T(8,128)(2,1)}, u32[]{:S(2)}) copy-start(bf16[32,2,16,128]{3,2,1,0:T(8,128)(2,1)} %get-tuple-element.8) | copy-start | bytes 786436

commit v3 on v2

--- a/solution.py
+++ b/solution.py
@@ -87,6 +87,8 @@
     rs,
     sel,
     bias,
+    key_mask,
+    eye,
     ret,
     ao,
     load_kv,
@@ -329,7 +331,8 @@
         stage1(i)
         return c
 
-    lax.fori_loop(0, KV_HEADS, start_item, 0)
+    window = 4
+    lax.fori_loop(0, window, start_item, 0)
 
     def msg_copy(k):
         peer = (g + k) % n_groups
@@ -580,56 +583,70 @@
 
         lax.fori_loop(1, n_groups, send, 0)
 
+    def prefill_masks():
+        shape = (n_tp * rows, rows)
+        key = lax.broadcasted_iota(jnp.int32, shape, 0)
+        row = lax.broadcasted_iota(jnp.int32, shape, 1) + t * rows
+        key_mask[...] = jnp.where(key <= row, 0.0, NEG).astype(jnp.bfloat16)
+        row = lax.broadcasted_iota(jnp.int32, (rows, rows), 0)
+        column = lax.broadcasted_iota(jnp.int32, (rows, rows), 1)
+        eye[...] = jnp.where(row == column, 1.0, 0.0).astype(jnp.bfloat16)
+
     def prefill_head(h):
         vis = span_offset[0] > 0
-        part = 4
+        part = 2
         n_rows = part * rows
-        kp = kv[h, 0].reshape(n_tp * rows, HEAD_DIM)
-        ks = kv[h, 1].reshape(n_tp * rows, HEAD_DIM)
-        vp = kv[h, 2].reshape(n_tp * rows, HEAD_DIM)
-        vs = kv[h, 3].reshape(n_tp * rows, HEAD_DIM)
-        position = lax.broadcasted_iota(jnp.int32, (n_rows, 1), 0) % rows + t * rows
-        key_ids = lax.broadcasted_iota(jnp.int32, (n_rows, n_tp * rows), 1)
+        n_keys = n_tp * rows
+        kp = kv[h, 0].reshape(n_keys, HEAD_DIM)
+        ks = jnp.concatenate([kv[h, 1].reshape(n_keys, HEAD_DIM), key_mask[...]], axis=1)
+        ones = jnp.ones((n_keys, HEAD_DIM), jnp.bfloat16)
+        vp = jnp.concatenate([kv[h, 2].reshape(n_keys, HEAD_DIM), ones], axis=1)
+        vs = jnp.concatenate([kv[h, 3].reshape(n_keys, HEAD_DIM), ones], axis=1)
+        position = lax.broadcasted_iota(jnp.int32, (n_rows, HEAD_DIM), 0) % rows + t * rows
         live = span_offset[0] + position < prompt_length[0]
-
-        def half(j, c):
-            def cols(i):
-                start = h * (GROUP_SIZE * HEAD_DIM) + (j * part + i) * HEAD_DIM
-                return pl.ds(pl.multiple_of(start, HEAD_DIM), HEAD_DIM)
-
-            q = jnp.concatenate([q_s[:, cols(i)] for i in range(part)], axis=0)
+        eyes = jnp.concatenate([eye[...]] * part, axis=0)
+
+        def cols(i):
+            start = h * (GROUP_SIZE * HEAD_DIM) + i * HEAD_DIM
+            return pl.ds(pl.multiple_of(start, HEAD_DIM), HEAD_DIM)
+
+        queries = [q_s[:, cols(i)] for i in range(GROUP_SIZE)]
+        for j in range(GROUP_SIZE // part):
+            q = jnp.concatenate(queries[j * part : (j + 1) * part], axis=0)
             sp = dot_t(q, kp)
-            ss = jnp.where(key_ids <= position, dot_t(q, ks), NEG)
+            ss = dot_t(jnp.concatenate([q, eyes], axis=1), ks)
             mp = jnp.max(sp, axis=1, keepdims=True)
             m = jnp.max(ss, axis=1, keepdims=True)
             m = jnp.where(vis, jnp.maximum(m, mp), m)
             wp = jnp.exp2((sp - jnp.where(vis, m, -NEG)) * RATE)
             ws = jnp.exp2((ss - m) * RATE)
-            total = jnp.sum(wp, axis=1, keepdims=True) + jnp.sum(ws, axis=1, keepdims=True)
             o = dot_n(wp.astype(jnp.bfloat16), vp) + dot_n(ws.astype(jnp.bfloat16), vs)
-            o = jnp.where(live, o / total, 0.0).astype(jnp.bfloat16)
+            o = o[:, :HEAD_DIM] / o[:, HEAD_DIM:]
+            o = jnp.where(live, o, 0.0).astype(jnp.bfloat16)
             for i in range(part):
-                q_s[:, cols(i)] = o[i * rows : (i + 1) * rows]
-            return c
-
-        lax.fori_loop(0, GROUP_SIZE // part, half, 0)
+                q_s[:, cols(j * part + i)] = o[i * rows : (i + 1) * rows]
 
     def head_out(h):
         width = GROUP_SIZE * HEAD_DIM
         cols = pl.ds(pl.multiple_of(h * width, width), width)
         return pltpu.make_async_copy(q_s.at[:, cols], p_out.at[:, cols], out_sem.at[h])
 
+    prefill_masks()
     decode()
     for h in range(3):
         stage_a(h)
+    stage_b(0)
     arrivals_choose()
-    for h in range(2):
-        stage_b(h)
+    stage_b(1)
     stage_c(0)
     stage_a(QUERY_ITEM)
     big[2].wait()
 
     def turn(s, c):
+        @pl.when(s + window < KV_HEADS)
+        def _():
+            start_item(s + window, 0)
+
         @pl.when(s + 3 < KV_HEADS)
         def _():
             stage_a(s + 3)
@@ -772,6 +789,8 @@
             pltpu.VMEM((n_tp, 4 * ROWS16, HEAD_DIM), f32),
             pltpu.VMEM((a_rows, slots * ROWS16), bf),
             pltpu.VMEM((a_rows, HEAD_DIM), f32),
+            pltpu.VMEM((n_tp * rows, rows), bf),
+            pltpu.VMEM((rows, rows), bf),
             pltpu.VMEM((n_groups, CAPACITY, ROWS16, HEAD_DIM), bf),
             pltpu.VMEM((n_groups, CAPACITY, ROWS16, HEAD_DIM), bf),
             dma((KV_HEADS, 4)),

time: 135 us -> 122 us (0.904)
  Pallas kernels: 128 us -> 115 us
    pallas_call x1, Pallas kernels: 128 us -> 115 us  [local(): pl.pallas_call(functools.partial(body, n_groups, n_tp), out_shape=(jax.Sh...]
where the time goes in v3:
time: 122 us
  Pallas kernels  115 us (94%)
  local copies, waits for them, and re-layouts  4.51 us (4%)
  between operations  1.95 us (2%)
    pallas_call x1, Pallas kernels, local(): pl.pallas_call(functools.partial(body, n_groups, n_tp), out_shape=(jax.Sh...  115 us
    unnamed x7, local copies, waits for them, and re-layouts  4.51 us

profile of v3, /device:TPU:8, one launch (start us, length us, event | category | flops | bytes accessed | tf_op | source)
XLA Modules:
  0.0 121.9 jit_solution(4532548143214255460)
XLA Ops:
  1.9 115.4 %shard_map.211 = (bf16[128,8192]{1,0:T(8,128)(2,1)}, bf16[512,128]{1,0:T(8,128)(2,1)}, bf16[32,2,16,128]{3,2,1,0:T(8,128)(2,1)}) custom-call(bf16[128,8192]{1,0:T(8,128)(2,1)} %pq.1, bf16[128,1024]{1,0:T(8,128)(2,1)} %sk.1, bf16[128,1024]{1,0:T(8,128)(2,1)} %sv.1, bf16[128,1024]{1,0:T(8,128)(2,1)} %pk.1, bf16[128,1024]{1,0:T(8,128)(2,1)} %pv.1, ...), custom_call_target="tpu_custom_call" | custom-call | tf_op jit(solution)/shard_map/pallas_call | solution.py:761
  117.4 0.0 copy-start.1
  117.4 0.0 copy-start
  117.4 3.1 %copy.32 = bf16[128,8192]{1,0:T(8,128)(2,1)} copy(bf16[128,8192]{1,0:T(8,128)(2,1)} %get-tuple-element.12) | data formatting | bytes 4194304
  120.5 0.0 copy-done.1
  120.5 0.7 copy.33
  121.2 0.0 copy-done
  121.2 0.7 copy.34
Async XLA Ops:
  117.4 3.2 %copy-start.1 = (bf16[512,128]{1,0:T(8,128)(2,1)S(1)}, bf16[512,128]{1,0:T(8,128)(2,1)}, u32[]{:S(2)}) copy-start(bf16[512,128]{1,0:T(8,128)(2,1)} %get-tuple-element.7) | copy-start | bytes 393220
  117.4 3.8 %copy-start = (bf16[32,2,16,128]{3,2,1,0:T(8,128)(2,1)S(1)}, bf16[32,2,16,128]{3,2,1,0:T(8,128)(2,1)}, u32[]{:S(2)}) copy-start(bf16[32,2,16,128]{3,2,1,0:T(8,128)(2,1)} %get-tuple-element.8) | copy-start | bytes 786436

commit v4 on v3

--- a/solution.py
+++ b/solution.py
@@ -19,6 +19,7 @@
 RATE = math.log2(math.e) / math.sqrt(HEAD_DIM)
 X_CHIPS = 4
 CORES = 2
+STAT_LANES = 16
 ITEMS = KV_HEADS + 1
 QUERY_ITEM = KV_HEADS
 
@@ -81,9 +82,15 @@
     rel,
     msg,
     rm,
-    po,
+    away,
+    away_stats,
+    home,
+    home_stats,
+    relayed,
+    relayed_stats,
+    landed,
+    landed_stats,
     ro,
-    ps,
     rs,
     sel,
     bias,
@@ -97,6 +104,8 @@
     x_recv,
     m_send,
     m_recv,
+    p_send,
+    p_recv,
     o_send,
     o_recv,
     s_send,
@@ -448,72 +457,133 @@
         keep = (col // local_len == quad_row) & ((col % local_len).astype(jnp.float32) < limit)
         bias[...] = jnp.where(keep, 0.0, NEG)
 
-    def po_copy(h, k):
+    def part_hop(src, dst, kind, device):
         return pltpu.make_async_remote_copy(
-            src_ref=po.at[h],
-            dst_ref=ro.at[t],
-            send_sem=o_send.at[k],
-            recv_sem=o_recv.at[t],
-            device_id={"tp": h},
+            src_ref=src,
+            dst_ref=dst,
+            send_sem=p_send.at[kind],
+            recv_sem=p_recv.at[kind],
+            device_id=device,
             device_id_type=MESH,
         )
 
-    def ps_copy(h, k):
-        return pltpu.make_async_remote_copy(
-            src_ref=ps.at[h],
-            dst_ref=rs.at[t],
-            send_sem=s_send.at[k],
-            recv_sem=s_recv.at[t],
-            device_id={"tp": h},
-            device_id_type=MESH,
-        )
-
-    def po_wait(k):
-        peer = (t + k) % n_tp
-        for send_sem, recv_sem, ref in ((o_send, o_recv, ro), (s_send, s_recv, rs)):
+    low, high = pl.ds(0, 2), pl.ds(2, 2)
+
+    def part_y():
+        return (
+            part_hop(away.at[low], relayed.at[low], 0, to_same),
+            part_hop(away.at[high], relayed.at[high], 1, to_cross),
+            part_hop(away_stats, relayed_stats, 2, to_cross),
+        )
+
+    def part_relay():
+        return (
+            part_hop(relayed.at[low], landed.at[low], 3, to_cross),
+            part_hop(relayed.at[high], landed.at[high], 4, to_same),
+            part_hop(relayed_stats, landed_stats, 5, to_same),
+        )
+
+    def x_peer(k):
+        return (x + k) % X_CHIPS
+
+    def part_x(k):
+        xs = x_peer(k)
+        device = {"tp": xs * 2 + yh}
+        out = []
+        for src, dst, send, recv in (
+            (home, ro, o_send, o_recv),
+            (home_stats, rs, s_send, s_recv),
+        ):
+            out.append(
+                pltpu.make_async_remote_copy(
+                    src_ref=src.at[xs],
+                    dst_ref=dst.at[x],
+                    send_sem=send.at[k],
+                    recv_sem=recv.at[x],
+                    device_id=device,
+                    device_id_type=MESH,
+                )
+            )
+        return out
+
+    def part_x_wait(k):
+        xs = x_peer(k)
+        for ref, send, recv in ((ro, o_send, o_recv), (rs, s_send, s_recv)):
             pltpu.make_async_remote_copy(
-                src_ref=ref.at[peer],
-                dst_ref=ref.at[peer],
-                send_sem=send_sem.at[k],
-                recv_sem=recv_sem.at[peer],
-                device_id={"tp": peer},
+                src_ref=ref.at[xs],
+                dst_ref=ref.at[xs],
+                send_sem=send.at[k],
+                recv_sem=recv.at[xs],
+                device_id={"tp": xs * 2 + yh},
                 device_id_type=MESH,
             ).wait_recv()
 
-    def partial_head(h, o_ref, s_ref, at):
-        cols = pl.ds(pl.multiple_of(h * HEAD_DIM, HEAD_DIM), HEAD_DIM)
-        lane = lax.broadcasted_iota(jnp.int32, (4 * ROWS16, HEAD_DIM), 1)
-        stats = jnp.zeros((4 * ROWS16, HEAD_DIM), jnp.float32)
-        for i in range(quads):
-            rows_i = slice(i * 4 * ROWS16, (i + 1) * 4 * ROWS16)
-            keys_i = slice(i * HEAD_DIM, (i + 1) * HEAD_DIM)
-            block, part = quad_rows(i)
-            q = kv[QUERY_ITEM, block, h // 2, h % 2, part, :]
-            s = dot_t(q, fk_s[keys_i, cols]) + bias[rows_i, :]
-            m = jnp.max(s, axis=1, keepdims=True)
-            w = jnp.exp2((s - m) * RATE)
-            total = jnp.sum(w, axis=1, keepdims=True)
-            o_ref[at, rows_i, :] = dot_n(w.astype(jnp.bfloat16), fv_s[keys_i, cols]).astype(
-                jnp.bfloat16
-            )
-            stats = jnp.where(lane == i, m, stats)
-            stats = jnp.where(lane == quads + i, total, stats)
-        s_ref[at] = stats
+    stat_lane = lax.broadcasted_iota(jnp.int32, (4 * ROWS16, HEAD_DIM), 1)
+
+    def partial_heads(ys, o_ref):
+        def one(xs, stats):
+            h = xs * 2 + ys
+            cols = pl.ds(pl.multiple_of(h * HEAD_DIM, HEAD_DIM), HEAD_DIM)
+            for i in range(quads):
+                rows_i = slice(i * 4 * ROWS16, (i + 1) * 4 * ROWS16)
+                keys_i = slice(i * HEAD_DIM, (i + 1) * HEAD_DIM)
+                block, part = quad_rows(i)
+                q = kv[QUERY_ITEM, block, xs, ys, part, :]
+                s = dot_t(q, fk_s[keys_i, cols]) + bias[rows_i, :]
+                m = jnp.max(s, axis=1, keepdims=True)
+                w = jnp.exp2((s - m) * RATE)
+                total = jnp.sum(w, axis=1, keepdims=True)
+                o_ref[xs, rows_i, :] = dot_n(w.astype(jnp.bfloat16), fv_s[keys_i, cols]).astype(
+                    jnp.bfloat16
+                )
+                at = xs * STAT_LANES + i
+                stats = jnp.where(stat_lane == at, m, stats)
+                stats = jnp.where(stat_lane == at + STAT_LANES // 2, total, stats)
+            return stats
+
+        return lax.fori_loop(
+            0, X_CHIPS, one, jnp.zeros((4 * ROWS16, HEAD_DIM), jnp.float32)
+        )
 
     def arrivals_partial():
         stage_d(QUERY_ITEM)
         big[3].wait()
         big[4].wait()
-
-        def one(k, c):
-            h = (t + k) % n_tp
-            partial_head(h, po, ps, h)
-            po_copy(h, k).start()
-            ps_copy(h, k).start()
-            return c
-
-        lax.fori_loop(1, n_tp, one, 0)
-        partial_head(t, ro, rs, t)
+        away_stats[...] = partial_heads(ny, away)
+        for copy in part_y():
+            copy.start()
+        home_stats[0] = partial_heads(yh, home)
+
+    def arrivals_relay():
+        for here, onward in zip(part_y(), part_relay()):
+            here.wait_recv()
+            onward.start()
+
+    def arrivals_pair():
+        for copy in part_relay():
+            copy.wait_recv()
+        mine = home_stats[0]
+        other = landed_stats[...]
+        m = jnp.maximum(mine, other)
+        w_mine = jnp.exp2((mine - m) * RATE)
+        w_other = jnp.exp2((other - m) * RATE)
+        half = STAT_LANES // 2
+        total = pltpu.roll(w_mine, half, 1) * mine + pltpu.roll(w_other, half, 1) * other
+        stats = jnp.where(stat_lane % STAT_LANES < half, m, total)
+        for xs in range(X_CHIPS):
+            for i in range(quads):
+                rows_i = slice(i * 4 * ROWS16, (i + 1) * 4 * ROWS16)
+                at = xs * STAT_LANES + i
+                o = home[xs, rows_i, :].astype(jnp.float32) * w_mine[:, at : at + 1]
+                o = o + landed[xs, rows_i, :].astype(jnp.float32) * w_other[:, at : at + 1]
+                home[xs, rows_i, :] = o.astype(jnp.bfloat16)
+            shift = (HEAD_DIM - xs * STAT_LANES) % HEAD_DIM
+            home_stats[xs] = stats if shift == 0 else pltpu.roll(stats, shift, 1)
+        for k in range(1, X_CHIPS):
+            for copy in part_x(k):
+                copy.start()
+        ro[x] = home[x]
+        rs[x] = home_stats[x]
 
     def ret_copy(k):
         peer = (g + k) % n_groups
@@ -538,11 +608,8 @@
         ).wait_recv()
 
     def arrivals_join():
-        def wait(k, c):
-            po_wait(k)
-            return c
-
-        lax.fori_loop(1, n_tp, wait, 0)
+        for k in range(1, X_CHIPS):
+            part_x_wait(k)
         slot_rows = n_groups * CAPACITY * ROWS16
         extra = rm[:, :, ROWS16 : 2 * ROWS16, :].reshape(slot_rows, HEAD_DIM)
         new = dot_n(sel[...], extra).reshape(n_prompts, ROWS16, HEAD_DIM)
@@ -552,8 +619,9 @@
         n1 = n1.reshape(a_rows, 1)
         ms = [
             jnp.concatenate([rs[p][:, i : i + 1] for i in range(quads)], axis=0)
-            for p in range(n_tp)
+            for p in range(X_CHIPS)
         ]
+        half = STAT_LANES // 2
         m = jnp.maximum(n0, n1)
         for mp in ms:
             m = jnp.maximum(m, mp)
@@ -561,10 +629,10 @@
         w1 = jnp.exp2((n1 - m) * RATE)
         total = w0 + w1
         o = jnp.zeros((a_rows, HEAD_DIM), jnp.float32)
-        for p in range(n_tp):
+        for p in range(X_CHIPS):
             wp = jnp.exp2((ms[p] - m) * RATE)
             lp = jnp.concatenate(
-                [rs[p][:, quads + i : quads + i + 1] for i in range(quads)], axis=0
+                [rs[p][:, half + i : half + i + 1] for i in range(quads)], axis=0
             )
             total = total + wp * lp
             o = o + wp * ro[p].astype(jnp.float32)
@@ -671,7 +739,15 @@
         def _():
             arrivals_partial()
 
-        @pl.when(s == 5)
+        @pl.when(s == 3)
+        def _():
+            arrivals_relay()
+
+        @pl.when(s == 4)
+        def _():
+            arrivals_pair()
+
+        @pl.when(s == 6)
         def _():
             arrivals_join()
 
@@ -695,18 +771,16 @@
         ret_copy(k).wait_send()
         return c
 
-    def drain_tp(k, c):
-        h = (t + k) % n_tp
-        po_copy(h, k).wait_send()
-        ps_copy(h, k).wait_send()
-        return c
-
     def drain_out(h, c):
         head_out(h).wait()
         return c
 
     lax.fori_loop(1, n_groups, drain_group, 0)
-    lax.fori_loop(1, n_tp, drain_tp, 0)
+    for copy in part_y() + part_relay():
+        copy.wait_send()
+    for k in range(1, X_CHIPS):
+        for copy in part_x(k):
+            copy.wait_send()
     lax.fori_loop(0, ITEMS, drain_item, 0)
     lax.fori_loop(0, KV_HEADS, drain_out, 0)
 
@@ -783,10 +857,16 @@
             pltpu.VMEM((ITEMS, 2, 2, X_CHIPS, rows, HEAD_DIM), bf),
             pltpu.VMEM((n_groups, CAPACITY, 2 * ROWS16, HEAD_DIM), bf),
             pltpu.VMEM((n_groups, CAPACITY, 2 * ROWS16, HEAD_DIM), bf),
-            pltpu.VMEM((n_tp, a_rows, HEAD_DIM), bf),
-            pltpu.VMEM((n_tp, a_rows, HEAD_DIM), bf),
-            pltpu.VMEM((n_tp, 4 * ROWS16, HEAD_DIM), f32),
-            pltpu.VMEM((n_tp, 4 * ROWS16, HEAD_DIM), f32),
+            pltpu.VMEM((X_CHIPS, a_rows, HEAD_DIM), bf),
+            pltpu.VMEM((4 * ROWS16, HEAD_DIM), f32),
+            pltpu.VMEM((X_CHIPS, a_rows, HEAD_DIM), bf),
+            pltpu.VMEM((X_CHIPS, 4 * ROWS16, HEAD_DIM), f32),
+            pltpu.VMEM((X_CHIPS, a_rows, HEAD_DIM), bf),
+            pltpu.VMEM((4 * ROWS16, HEAD_DIM), f32),
+            pltpu.VMEM((X_CHIPS, a_rows, HEAD_DIM), bf),
+            pltpu.VMEM((4 * ROWS16, HEAD_DIM), f32),
+            pltpu.VMEM((X_CHIPS, a_rows, HEAD_DIM), bf),
+            pltpu.VMEM((X_CHIPS, 4 * ROWS16, HEAD_DIM), f32),
             pltpu.VMEM((a_rows, slots * ROWS16), bf),
             pltpu.VMEM((a_rows, HEAD_DIM), f32),
             pltpu.VMEM((n_tp * rows, rows), bf),
@@ -799,10 +879,12 @@
             dma((ITEMS, 10)),
             dma((n_groups,)),
             dma((n_groups,)),
-            dma((n_tp,)),
-            dma((n_tp,)),
-            dma((n_tp,)),
-            dma((n_tp,)),
+            dma((6,)),
+            dma((6,)),
+            dma((X_CHIPS,)),
+            dma((X_CHIPS,)),
+            dma((X_CHIPS,)),
+            dma((X_CHIPS,)),
             dma((n_groups,)),
             dma((n_groups,)),
             dma((KV_HEADS,)),

time: 122 us -> 126 us (1.033); the launches traced: 122 us -> 124 us
  Pallas kernels: 115 us -> 118 us
    pallas_call x1, Pallas kernels: 115 us -> 118 us  [local(): pl.pallas_call(functools.partial(body, n_groups, n_tp), out_shape=(jax.Sh...]
where the time goes in v4:
time: 126 us; the launch traced here: 124 us
  Pallas kernels  118 us (94%)
  local copies, waits for them, and re-layouts  4.51 us (4%)
  between operations  1.95 us (2%)
    pallas_call x1, Pallas kernels, local(): pl.pallas_call(functools.partial(body, n_groups, n_tp), out_shape=(jax.Sh...  118 us
    unnamed x7, local copies, waits for them, and re-layouts  4.51 us

profile of v4, /device:TPU:8, one launch (start us, length us, event | category | flops | bytes accessed | tf_op | source)
XLA Modules:
  0.0 124.1 jit_solution(4879984679960630268)
XLA Ops:
  1.9 117.6 %shard_map.211 = (bf16[128,8192]{1,0:T(8,128)(2,1)}, bf16[512,128]{1,0:T(8,128)(2,1)}, bf16[32,2,16,128]{3,2,1,0:T(8,128)(2,1)}) custom-call(bf16[128,8192]{1,0:T(8,128)(2,1)} %pq.1, bf16[128,1024]{1,0:T(8,128)(2,1)} %sk.1, bf16[128,1024]{1,0:T(8,128)(2,1)} %sv.1, bf16[128,1024]{1,0:T(8,128)(2,1)} %pk.1, bf16[128,1024]{1,0:T(8,128)(2,1)} %pv.1, ...), custom_call_target="tpu_custom_call" | custom-call | tf_op jit(solution)/shard_map/pallas_call | solution.py:835
  119.6 0.0 copy-start.1
  119.6 0.0 copy-start
  119.6 3.1 %copy.32 = bf16[128,8192]{1,0:T(8,128)(2,1)} copy(bf16[128,8192]{1,0:T(8,128)(2,1)} %get-tuple-element.12) | data formatting | bytes 4194304
  122.7 0.0 copy-done.1
  122.7 0.7 copy.33
  123.4 0.0 copy-done
  123.4 0.7 copy.34
Async XLA Ops:
  119.6 3.2 %copy-start.1 = (bf16[512,128]{1,0:T(8,128)(2,1)S(1)}, bf16[512,128]{1,0:T(8,128)(2,1)}, u32[]{:S(2)}) copy-start(bf16[512,128]{1,0:T(8,128)(2,1)} %get-tuple-element.7) | copy-start | bytes 393220
  119.6 3.8 %copy-start = (bf16[32,2,16,128]{3,2,1,0:T(8,128)(2,1)S(1)}, bf16[32,2,16,128]{3,2,1,0:T(8,128)(2,1)}, u32[]{:S(2)}) copy-start(bf16[32,2,16,128]{3,2,1,0:T(8,128)(2,1)} %get-tuple-element.8) | copy-start | bytes 786436

commit v5 on v3

--- a/solution.py
+++ b/solution.py
@@ -107,14 +107,14 @@
 ):
     g = lax.axis_index("group")
     t = lax.axis_index("tp")
-    x, yh = t // 2, t % 2
-    right = ((x + 1) % X_CHIPS) * 2 + yh
-    left = ((x + X_CHIPS - 1) % X_CHIPS) * 2 + yh
+    x, yh = t >> 1, t & 1
+    right = ((x + 1) & (X_CHIPS - 1)) * 2 + yh
+    left = ((x + X_CHIPS - 1) & (X_CHIPS - 1)) * 2 + yh
     partner = x * 2 + (1 - yh)
-    right_x = (x + 1) % X_CHIPS
-    left_x = (x + X_CHIPS - 1) % X_CHIPS
-    far_x = (x + 2) % X_CHIPS
-    yl = (g // CORES) % 2
+    right_x = (x + 1) & (X_CHIPS - 1)
+    left_x = (x + X_CHIPS - 1) & (X_CHIPS - 1)
+    far_x = (x + 2) & (X_CHIPS - 1)
+    yl = (g // CORES) & 1
     beside = g + CORES * (1 - 2 * yl)
     local_len = HEAD_DIM // 4
     n_prompts = fk_s.shape[0] // local_len
@@ -147,12 +147,12 @@
 
     def greet_group(k, c):
         pl.semaphore_signal(
-            barrier, inc=1, device_id={"group": (g + k) % n_groups}, device_id_type=MESH
+            barrier, inc=1, device_id={"group": (g + k) & (n_groups - 1)}, device_id_type=MESH
         )
         return c
 
     def greet_tp(k, c):
-        pl.semaphore_signal(barrier, inc=1, device_id={"tp": (t + k) % n_tp}, device_id_type=MESH)
+        pl.semaphore_signal(barrier, inc=1, device_id={"tp": (t + k) & (n_tp - 1)}, device_id_type=MESH)
         return c
 
     lax.fori_loop(1, n_groups, greet_group, 0)
@@ -167,7 +167,7 @@
     ny = 1 - yh
 
     def y_first(i):
-        return i % 3 != 1
+        return (i & 1 == 1) | (i == 0) | (i == QUERY_ITEM)
 
     def hop(src, dst, kind, i, device):
         return pltpu.make_async_remote_copy(
@@ -331,11 +331,11 @@
         stage1(i)
         return c
 
-    window = 4
-    lax.fori_loop(0, window, start_item, 0)
+    start_item(0, 0)
+    start_item(1, 0)
 
     def msg_copy(k):
-        peer = (g + k) % n_groups
+        peer = (g + k) & (n_groups - 1)
         return pltpu.make_async_remote_copy(
             src_ref=msg.at[peer],
             dst_ref=rm.at[g],
@@ -346,7 +346,7 @@
         )
 
     def msg_wait(k):
-        peer = (g + k) % n_groups
+        peer = (g + k) & (n_groups - 1)
         pltpu.make_async_remote_copy(
             src_ref=rm.at[peer],
             dst_ref=rm.at[peer],
@@ -469,7 +469,7 @@
         )
 
     def po_wait(k):
-        peer = (t + k) % n_tp
+        peer = (t + k) & (n_tp - 1)
         for send_sem, recv_sem, ref in ((o_send, o_recv, ro), (s_send, s_recv, rs)):
             pltpu.make_async_remote_copy(
                 src_ref=ref.at[peer],
@@ -488,7 +488,7 @@
             rows_i = slice(i * 4 * ROWS16, (i + 1) * 4 * ROWS16)
             keys_i = slice(i * HEAD_DIM, (i + 1) * HEAD_DIM)
             block, part = quad_rows(i)
-            q = kv[QUERY_ITEM, block, h // 2, h % 2, part, :]
+            q = kv[QUERY_ITEM, block, h >> 1, h & 1, part, :]
             s = dot_t(q, fk_s[keys_i, cols]) + bias[rows_i, :]
             m = jnp.max(s, axis=1, keepdims=True)
             w = jnp.exp2((s - m) * RATE)
@@ -506,7 +506,7 @@
         big[4].wait()
 
         def one(k, c):
-            h = (t + k) % n_tp
+            h = (t + k) & (n_tp - 1)
             partial_head(h, po, ps, h)
             po_copy(h, k).start()
             ps_copy(h, k).start()
@@ -516,7 +516,7 @@
         partial_head(t, ro, rs, t)
 
     def ret_copy(k):
-        peer = (g + k) % n_groups
+        peer = (g + k) & (n_groups - 1)
         return pltpu.make_async_remote_copy(
             src_ref=ret.at[peer],
             dst_ref=ao.at[g],
@@ -527,7 +527,7 @@
         )
 
     def ret_wait(k):
-        peer = (g + k) % n_groups
+        peer = (g + k) & (n_groups - 1)
         pltpu.make_async_remote_copy(
             src_ref=ao.at[peer],
             dst_ref=ao.at[peer],
@@ -592,7 +592,7 @@
         column = lax.broadcasted_iota(jnp.int32, (rows, rows), 1)
         eye[...] = jnp.where(row == column, 1.0, 0.0).astype(jnp.bfloat16)
 
-    def prefill_head(h):
+    def prefill_half(h, half):
         vis = span_offset[0] > 0
         part = 2
         n_rows = part * rows
@@ -607,11 +607,11 @@
         eyes = jnp.concatenate([eye[...]] * part, axis=0)
 
         def cols(i):
-            start = h * (GROUP_SIZE * HEAD_DIM) + i * HEAD_DIM
+            start = (2 * h + half) * (GROUP_SIZE // 2 * HEAD_DIM) + i * HEAD_DIM
             return pl.ds(pl.multiple_of(start, HEAD_DIM), HEAD_DIM)
 
-        queries = [q_s[:, cols(i)] for i in range(GROUP_SIZE)]
-        for j in range(GROUP_SIZE // part):
+        queries = [q_s[:, cols(i)] for i in range(GROUP_SIZE // 2)]
+        for j in range(GROUP_SIZE // 2 // part):
             q = jnp.concatenate(queries[j * part : (j + 1) * part], axis=0)
             sp = dot_t(q, kp)
             ss = dot_t(jnp.concatenate([q, eyes], axis=1), ks)
@@ -632,55 +632,73 @@
         return pltpu.make_async_copy(q_s.at[:, cols], p_out.at[:, cols], out_sem.at[h])
 
     prefill_masks()
+    for h in (0, 1):
+        stage_a(h)
+    for h in (0, 1):
+        stage_b(h)
+    start_item(2, 0)
     decode()
-    for h in range(3):
-        stage_a(h)
-    stage_b(0)
+    stage_c(0)
+    stage_c(1)
+    start_item(3, 0)
     arrivals_choose()
-    stage_b(1)
-    stage_c(0)
+    stage_a(2)
+    stage_a(3)
+    start_item(4, 0)
+    stage_b(2)
     stage_a(QUERY_ITEM)
     big[2].wait()
 
-    def turn(s, c):
-        @pl.when(s + window < KV_HEADS)
+    def half_turn(n, c):
+        s = n >> 1
+
+        @pl.when(n & 1 == 0)
         def _():
-            start_item(s + window, 0)
-
-        @pl.when(s + 3 < KV_HEADS)
+            stage_d(s)
+
+        @pl.when(n & 1 == 1)
         def _():
-            stage_a(s + 3)
-
-        @pl.when(s + 2 < KV_HEADS)
+            @pl.when(s + 2 < KV_HEADS)
+            def _():
+                stage_c(s + 2)
+
+            @pl.when(s + 3 < KV_HEADS)
+            def _():
+                stage_b(s + 3)
+
+            @pl.when(s + 4 < KV_HEADS)
+            def _():
+                stage_a(s + 4)
+
+            @pl.when(s + 5 < KV_HEADS)
+            def _():
+                start_item(s + 5, 0)
+
+            @pl.when(s == 0)
+            def _():
+                stage_b(QUERY_ITEM)
+
+            @pl.when(s == 1)
+            def _():
+                stage_c(QUERY_ITEM)
+
+            @pl.when(s == 2)
+            def _():
+                arrivals_partial()
+
+            @pl.when(s == 5)
+            def _():
+                arrivals_join()
+
+        prefill_half(s, n & 1)
+
+        @pl.when(n & 1 == 1)
         def _():
-            stage_b(s + 2)
-
-        @pl.when(s + 1 < KV_HEADS)
-        def _():
-            stage_c(s + 1)
-
-        @pl.when(s == 0)
-        def _():
-            stage_b(QUERY_ITEM)
-
-        @pl.when(s == 1)
-        def _():
-            stage_c(QUERY_ITEM)
-
-        @pl.when(s == 2)
-        def _():
-            arrivals_partial()
-
-        @pl.when(s == 5)
-        def _():
-            arrivals_join()
-
-        stage_d(s)
-        prefill_head(s)
-        head_out(s).start()
-        return c
-
-    lax.fori_loop(0, KV_HEADS, turn, 0)
+            head_out(s).start()
+
+        return c
+
+    lax.fori_loop(0, 2 * KV_HEADS, half_turn, 0)
 
     def wait_ret(k, c):
         ret_wait(k)
@@ -696,7 +714,7 @@
         return c
 
     def drain_tp(k, c):
-        h = (t + k) % n_tp
+        h = (t + k) & (n_tp - 1)
         po_copy(h, k).wait_send()
         ps_copy(h, k).wait_send()
         return c
@@ -709,6 +727,34 @@
     lax.fori_loop(1, n_tp, drain_tp, 0)
     lax.fori_loop(0, ITEMS, drain_item, 0)
     lax.fori_loop(0, KV_HEADS, drain_out, 0)
+
+
+def publish_body(*refs):
+    sources, results, sems = refs[:3], refs[3:6], refs[6]
+    copies = []
+    parts = 8
+    width = sources[0].shape[1] // parts
+    for i in range(parts):
+        cols = slice(i * width, (i + 1) * width)
+        copies.append((sources[0].at[:, cols], results[0].at[:, cols]))
+    copies += [(sources[1], results[1]), (sources[2], results[2])]
+    copies = [pltpu.make_async_copy(a, b, sems.at[i]) for i, (a, b) in enumerate(copies)]
+    for copy in copies:
+        copy.start()
+    for copy in copies:
+        copy.wait()
+
+
+def publish(*results):
+    any_ = pl.BlockSpec(memory_space=pl.ANY)
+    return pl.pallas_call(
+        publish_body,
+        out_shape=tuple(jax.ShapeDtypeStruct(r.shape, r.dtype) for r in results),
+        in_specs=[any_] * 3,
+        out_specs=[any_] * 3,
+        scratch_shapes=[pltpu.SemaphoreType.DMA((10,))],
+        compiler_params=pltpu.CompilerParams(vmem_limit_bytes=56 * 1024 * 1024),
+    )(*results)
 
 
 def to_rows(queries):
@@ -832,6 +878,7 @@
         arrival_new_keys,
         arrival_new_values,
     )
+    p_out, d_out, a_out = publish(p_out, d_out, a_out)
     return (p_out, from_rows(d_out, dec), from_rows(a_out, slots))
 
 

time: 122 us -> 204 us (1.67)
  Pallas kernels: 115 us -> 200 us
  local copies, waits for them, and re-layouts: 4.51 us -> 0 us
    pallas_call x0 -> x1, Pallas kernels: none -> 76.6 us  [publish(): pl.pallas_call(publish_body, out_shape=tuple((jax.ShapeDtypeStruct(r.shap...]
    pallas_call x1, Pallas kernels: 115 us -> 123 us  [local(): pl.pallas_call(functools.partial(body, n_groups, n_tp), out_shape=(jax.Sh...]
    unnamed x7 -> x0, local copies, waits for them, and re-layouts: 4.51 us -> none
where the time goes in v5:
time: 204 us; the launch traced here: 202 us
  Pallas kernels  200 us (98%)
    pallas_call x1, Pallas kernels, local(): pl.pallas_call(functools.partial(body, n_groups, n_tp), out_shape=(jax.Sh...  123 us
    pallas_call x1, Pallas kernels, publish(): pl.pallas_call(publish_body, out_shape=tuple((jax.ShapeDtypeStruct(r.shap...  76.6 us

profile of v5, /device:TPU:8, one launch (start us, length us, event | category | flops | bytes accessed | tf_op | source)
XLA Modules:
  0.0 202.1 jit_solution(4680964319077281596)
XLA Ops:
  1.9 123.5 %shard_map.211 = (bf16[128,8192]{1,0:T(8,128)(2,1)}, bf16[512,128]{1,0:T(8,128)(2,1)}, bf16[32,2,16,128]{3,2,1,0:T(8,128)(2,1)}) custom-call(bf16[128,8192]{1,0:T(8,128)(2,1)} %pq.1, bf16[128,1024]{1,0:T(8,128)(2,1)} %sk.1, bf16[128,1024]{1,0:T(8,128)(2,1)} %sv.1, bf16[128,1024]{1,0:T(8,128)(2,1)} %pk.1, bf16[128,1024]{1,0:T(8,128)(2,1)} %pv.1, ...), custom_call_target="tpu_custom_call" | custom-call | tf_op jit(solution)/shard_map/pallas_call | solution.py:807
  125.4 76.6 %shard_map.212 = (bf16[128,8192]{1,0:T(8,128)(2,1)}, bf16[512,128]{1,0:T(8,128)(2,1)}, bf16[32,2,16,128]{3,2,1,0:T(8,128)(2,1)}) custom-call(bf16[128,8192]{1,0:T(8,128)(2,1)} %get-tuple-element.9.refs_0_, bf16[512,128]{1,0:T(8,128)(2,1)} %get-tuple-element.10.refs_1_, bf16[32,2,16,128]{3,2,1,0:T(8,128)(2,1)} %get-tuple-element.11.refs_2_), custom_call_target="tpu_custom_call" | custom-call | tf_op jit(solution)/shard_map/pallas_call | solution.py:750

commit v6 on v3

--- a/solution.py
+++ b/solution.py
@@ -19,6 +19,7 @@
 RATE = math.log2(math.e) / math.sqrt(HEAD_DIM)
 X_CHIPS = 4
 CORES = 2
+STAT_LANES = 16
 ITEMS = KV_HEADS + 1
 QUERY_ITEM = KV_HEADS
 
@@ -107,14 +108,14 @@
 ):
     g = lax.axis_index("group")
     t = lax.axis_index("tp")
-    x, yh = t // 2, t % 2
-    right = ((x + 1) % X_CHIPS) * 2 + yh
-    left = ((x + X_CHIPS - 1) % X_CHIPS) * 2 + yh
+    x, yh = t >> 1, t & 1
+    right = ((x + 1) & (X_CHIPS - 1)) * 2 + yh
+    left = ((x + X_CHIPS - 1) & (X_CHIPS - 1)) * 2 + yh
     partner = x * 2 + (1 - yh)
-    right_x = (x + 1) % X_CHIPS
-    left_x = (x + X_CHIPS - 1) % X_CHIPS
-    far_x = (x + 2) % X_CHIPS
-    yl = (g // CORES) % 2
+    right_x = (x + 1) & (X_CHIPS - 1)
+    left_x = (x + X_CHIPS - 1) & (X_CHIPS - 1)
+    far_x = (x + 2) & (X_CHIPS - 1)
+    yl = (g // CORES) & 1
     beside = g + CORES * (1 - 2 * yl)
     local_len = HEAD_DIM // 4
     n_prompts = fk_s.shape[0] // local_len
@@ -126,7 +127,7 @@
 
     def kv_load(h, a):
         cols = pl.ds(pl.multiple_of(h * HEAD_DIM, HEAD_DIM), HEAD_DIM)
-        return pltpu.make_async_copy(arrays[a].at[:, cols], kv.at[h, a, x, yh], load_kv.at[h, a])
+        return pltpu.make_async_copy(arrays[a].at[:, cols], kv.at[h, a, x, yh], load_kv.at[h])
 
     def start_loads(h, c):
         for a in range(4):
@@ -147,12 +148,12 @@
 
     def greet_group(k, c):
         pl.semaphore_signal(
-            barrier, inc=1, device_id={"group": (g + k) % n_groups}, device_id_type=MESH
+            barrier, inc=1, device_id={"group": (g + k) & (n_groups - 1)}, device_id_type=MESH
         )
         return c
 
     def greet_tp(k, c):
-        pl.semaphore_signal(barrier, inc=1, device_id={"tp": (t + k) % n_tp}, device_id_type=MESH)
+        pl.semaphore_signal(barrier, inc=1, device_id={"tp": (t + k) & (n_tp - 1)}, device_id_type=MESH)
         return c
 
     lax.fori_loop(1, n_groups, greet_group, 0)
@@ -326,42 +327,40 @@
         return c
 
     def start_item(i, c):
-        for a in range(4):
-            kv_load(i, a).wait()
+        block = kv.at[i, :, x, yh]
+        pltpu.make_async_copy(block, block, load_kv.at[i]).wait()
         stage1(i)
         return c
 
     window = 4
     lax.fori_loop(0, window, start_item, 0)
 
-    def msg_copy(k):
-        peer = (g + k) % n_groups
+    others = pl.ds(0, n_groups - 1)
+
+    def group_copy(src, dst, send_sem, recv_sem, peer):
         return pltpu.make_async_remote_copy(
-            src_ref=msg.at[peer],
-            dst_ref=rm.at[g],
-            send_sem=m_send.at[k],
-            recv_sem=m_recv.at[g],
+            src_ref=src,
+            dst_ref=dst,
+            send_sem=send_sem,
+            recv_sem=recv_sem,
             device_id={"group": peer},
             device_id_type=MESH,
         )
 
-    def msg_wait(k):
-        peer = (g + k) % n_groups
-        pltpu.make_async_remote_copy(
-            src_ref=rm.at[peer],
-            dst_ref=rm.at[peer],
-            send_sem=m_send.at[k],
-            recv_sem=m_recv.at[peer],
-            device_id={"group": peer},
-            device_id_type=MESH,
-        ).wait_recv()
+    def all_msgs():
+        return group_copy(msg.at[others], rm.at[others], m_send, m_recv, beside)
+
+    def all_rets():
+        return group_copy(ret.at[others], ao.at[others], b_send, b_recv, beside)
 
     def send_msg(k, c):
-        msg_copy(k).start()
-        return c
-
-    def wait_msg(k, c):
-        msg_wait(k)
+        peer = (g + k) & (n_groups - 1)
+        group_copy(msg.at[peer], rm.at[g], m_send, m_recv, peer).start()
+        return c
+
+    def send_ret(k, c):
+        peer = (g + k) & (n_groups - 1)
+        group_copy(ret.at[peer], ao.at[g], b_send, b_recv, peer).start()
         return c
 
     pair = (n_groups, CAPACITY, ROWS16, HEAD_DIM)
@@ -417,7 +416,7 @@
         return jnp.concatenate(parts, axis=0)
 
     def arrivals_choose():
-        lax.fori_loop(1, n_groups, wait_msg, 0)
+        all_msgs().wait_recv()
         lanes = routes.shape[1]
         per_row = lanes // n_prompts
         base = g % per_row * n_prompts
@@ -469,7 +468,7 @@
         )
 
     def po_wait(k):
-        peer = (t + k) % n_tp
+        peer = (t + k) & (n_tp - 1)
         for send_sem, recv_sem, ref in ((o_send, o_recv, ro), (s_send, s_recv, rs)):
             pltpu.make_async_remote_copy(
                 src_ref=ref.at[peer],
@@ -484,20 +483,24 @@
         cols = pl.ds(pl.multiple_of(h * HEAD_DIM, HEAD_DIM), HEAD_DIM)
         lane = lax.broadcasted_iota(jnp.int32, (4 * ROWS16, HEAD_DIM), 1)
         stats = jnp.zeros((4 * ROWS16, HEAD_DIM), jnp.float32)
+        rows_of = [slice(i * 4 * ROWS16, (i + 1) * 4 * ROWS16) for i in range(quads)]
+        keys_of = [slice(i * HEAD_DIM, (i + 1) * HEAD_DIM) for i in range(quads)]
+        scores = []
         for i in range(quads):
-            rows_i = slice(i * 4 * ROWS16, (i + 1) * 4 * ROWS16)
-            keys_i = slice(i * HEAD_DIM, (i + 1) * HEAD_DIM)
             block, part = quad_rows(i)
-            q = kv[QUERY_ITEM, block, h // 2, h % 2, part, :]
-            s = dot_t(q, fk_s[keys_i, cols]) + bias[rows_i, :]
-            m = jnp.max(s, axis=1, keepdims=True)
-            w = jnp.exp2((s - m) * RATE)
-            total = jnp.sum(w, axis=1, keepdims=True)
-            o_ref[at, rows_i, :] = dot_n(w.astype(jnp.bfloat16), fv_s[keys_i, cols]).astype(
-                jnp.bfloat16
-            )
-            stats = jnp.where(lane == i, m, stats)
-            stats = jnp.where(lane == quads + i, total, stats)
+            q = kv[QUERY_ITEM, block, h >> 1, h & 1, part, :]
+            scores.append(dot_t(q, fk_s[keys_of[i], cols]))
+        scores = [s + bias[r, :] for s, r in zip(scores, rows_of)]
+        tops = [jnp.max(s, axis=1, keepdims=True) for s in scores]
+        weights = [jnp.exp2((s - m) * RATE) for s, m in zip(scores, tops)]
+        totals = [jnp.sum(w, axis=1, keepdims=True) for w in weights]
+        outs = [
+            dot_n(w.astype(jnp.bfloat16), fv_s[k, cols]) for w, k in zip(weights, keys_of)
+        ]
+        for i in range(quads):
+            o_ref[at, rows_of[i], :] = outs[i].astype(jnp.bfloat16)
+            stats = jnp.where(lane == i, tops[i], stats)
+            stats = jnp.where(lane == STAT_LANES // 2 + i, totals[i], stats)
         s_ref[at] = stats
 
     def arrivals_partial():
@@ -506,7 +509,7 @@
         big[4].wait()
 
         def one(k, c):
-            h = (t + k) % n_tp
+            h = (t + k) & (n_tp - 1)
             partial_head(h, po, ps, h)
             po_copy(h, k).start()
             ps_copy(h, k).start()
@@ -514,28 +517,6 @@
 
         lax.fori_loop(1, n_tp, one, 0)
         partial_head(t, ro, rs, t)
-
-    def ret_copy(k):
-        peer = (g + k) % n_groups
-        return pltpu.make_async_remote_copy(
-            src_ref=ret.at[peer],
-            dst_ref=ao.at[g],
-            send_sem=b_send.at[k],
-            recv_sem=b_recv.at[g],
-            device_id={"group": peer},
-            device_id_type=MESH,
-        )
-
-    def ret_wait(k):
-        peer = (g + k) % n_groups
-        pltpu.make_async_remote_copy(
-            src_ref=ao.at[peer],
-            dst_ref=ao.at[peer],
-            send_sem=b_send.at[k],
-            recv_sem=b_recv.at[peer],
-            device_id={"group": peer},
-            device_id_type=MESH,
-        ).wait_recv()
 
     def arrivals_join():
         def wait(k, c):
@@ -550,38 +531,46 @@
         n0, n1 = new_scores(q3, (new[:, 0:1], new[:, 1:2]))
         n0 = n0.reshape(a_rows, 1)
         n1 = n1.reshape(a_rows, 1)
-        ms = [
-            jnp.concatenate([rs[p][:, i : i + 1] for i in range(quads)], axis=0)
-            for p in range(n_tp)
-        ]
-        m = jnp.maximum(n0, n1)
-        for mp in ms:
-            m = jnp.maximum(m, mp)
-        w0 = jnp.exp2((n0 - m) * RATE)
-        w1 = jnp.exp2((n1 - m) * RATE)
+        tile = (4 * ROWS16, HEAD_DIM)
+        lane = lax.broadcasted_iota(jnp.int32, tile, 1)
+        rows_of = [slice(i * 4 * ROWS16, (i + 1) * 4 * ROWS16) for i in range(quads)]
+        t0 = jnp.full(tile, NEG, jnp.float32)
+        t1 = jnp.full(tile, NEG, jnp.float32)
+        for i in range(quads):
+            t0 = jnp.where(lane == i, n0[rows_of[i]], t0)
+            t1 = jnp.where(lane == i, n1[rows_of[i]], t1)
+        live = lane < quads
+        stats = [rs[p] for p in range(n_tp)]
+        tops = [jnp.where(live, st, NEG) for st in stats]
+        m = jnp.maximum(t0, t1)
+        for top in tops:
+            m = jnp.maximum(m, top)
+        w0 = jnp.exp2((t0 - m) * RATE)
+        w1 = jnp.exp2((t1 - m) * RATE)
         total = w0 + w1
-        o = jnp.zeros((a_rows, HEAD_DIM), jnp.float32)
-        for p in range(n_tp):
-            wp = jnp.exp2((ms[p] - m) * RATE)
-            lp = jnp.concatenate(
-                [rs[p][:, quads + i : quads + i + 1] for i in range(quads)], axis=0
-            )
-            total = total + wp * lp
-            o = o + wp * ro[p].astype(jnp.float32)
-        w0 = w0.astype(jnp.bfloat16).astype(jnp.float32).reshape(n_prompts, ROWS16, 1)
-        w1 = w1.astype(jnp.bfloat16).astype(jnp.float32).reshape(n_prompts, ROWS16, 1)
-        o = o + (w0 * new[:, 2:3] + w1 * new[:, 3:4]).reshape(a_rows, HEAD_DIM)
-        res = (o / total).astype(jnp.bfloat16)
+        weights = [jnp.exp2((top - m) * RATE) for top in tops]
+        for w, st in zip(weights, stats):
+            total = total + w * pltpu.roll(st, HEAD_DIM - STAT_LANES // 2, 1)
+        inverse = 1.0 / jnp.where(live, total, 1.0)
+        weights = [w * inverse for w in weights]
+        w0 = w0.astype(jnp.bfloat16).astype(jnp.float32) * inverse
+        w1 = w1.astype(jnp.bfloat16).astype(jnp.float32) * inverse
+        parts = []
+        for i in range(quads):
+            wide = (4, ROWS16, HEAD_DIM)
+            v0 = jnp.broadcast_to(new[4 * i : 4 * i + 4, 2:3], wide).reshape(tile)
+            v1 = jnp.broadcast_to(new[4 * i : 4 * i + 4, 3:4], wide).reshape(tile)
+            o = w0[:, i : i + 1] * v0 + w1[:, i : i + 1] * v1
+            for p in range(n_tp):
+                o = o + weights[p][:, i : i + 1] * ro[p, rows_of[i], :].astype(jnp.float32)
+            parts.append(o.astype(jnp.bfloat16))
+        res = jnp.concatenate(parts, axis=0)
         back = lax.dot_general(
             sel[...], res, (((0,), (0,)), ((), ())), preferred_element_type=jnp.float32
         )
         ret[...] = back.astype(jnp.bfloat16).reshape(n_groups, CAPACITY, ROWS16, HEAD_DIM)
 
-        def send(k, c):
-            ret_copy(k).start()
-            return c
-
-        lax.fori_loop(1, n_groups, send, 0)
+        lax.fori_loop(1, n_groups, send_ret, 0)
 
     def prefill_masks():
         shape = (n_tp * rows, rows)
@@ -611,10 +600,17 @@
             return pl.ds(pl.multiple_of(start, HEAD_DIM), HEAD_DIM)
 
         queries = [q_s[:, cols(i)] for i in range(GROUP_SIZE)]
-        for j in range(GROUP_SIZE // part):
+        chains = GROUP_SIZE // part
+
+        def scores_of(j):
             q = jnp.concatenate(queries[j * part : (j + 1) * part], axis=0)
-            sp = dot_t(q, kp)
-            ss = dot_t(jnp.concatenate([q, eyes], axis=1), ks)
+            return dot_t(q, kp), dot_t(jnp.concatenate([q, eyes], axis=1), ks)
+
+        ahead = scores_of(0)
+        for j in range(chains):
+            sp, ss = ahead
+            if j + 1 < chains:
+                ahead = scores_of(j + 1)
             mp = jnp.max(sp, axis=1, keepdims=True)
             m = jnp.max(ss, axis=1, keepdims=True)
             m = jnp.where(vis, jnp.maximum(m, mp), m)
@@ -682,21 +678,12 @@
 
     lax.fori_loop(0, KV_HEADS, turn, 0)
 
-    def wait_ret(k, c):
-        ret_wait(k)
-        return c
-
-    lax.fori_loop(1, n_groups, wait_ret, 0)
+    all_rets().wait_recv()
     ao[g] = ret[g]
     a_out[...] = ao[...]
 
-    def drain_group(k, c):
-        msg_copy(k).wait_send()
-        ret_copy(k).wait_send()
-        return c
-
     def drain_tp(k, c):
-        h = (t + k) % n_tp
+        h = (t + k) & (n_tp - 1)
         po_copy(h, k).wait_send()
         ps_copy(h, k).wait_send()
         return c
@@ -705,7 +692,8 @@
         head_out(h).wait()
         return c
 
-    lax.fori_loop(1, n_groups, drain_group, 0)
+    all_msgs().wait_send()
+    all_rets().wait_send()
     lax.fori_loop(1, n_tp, drain_tp, 0)
     lax.fori_loop(0, ITEMS, drain_item, 0)
     lax.fori_loop(0, KV_HEADS, drain_out, 0)
@@ -793,18 +781,18 @@
             pltpu.VMEM((rows, rows), bf),
             pltpu.VMEM((n_groups, CAPACITY, ROWS16, HEAD_DIM), bf),
             pltpu.VMEM((n_groups, CAPACITY, ROWS16, HEAD_DIM), bf),
-            dma((KV_HEADS, 4)),
+            dma((KV_HEADS,)),
             dma((5,)),
             dma((ITEMS, 10)),
             dma((ITEMS, 10)),
-            dma((n_groups,)),
-            dma((n_groups,)),
+            dma(()),
+            dma(()),
             dma((n_tp,)),
             dma((n_tp,)),
             dma((n_tp,)),
             dma((n_tp,)),
-            dma((n_groups,)),
-            dma((n_groups,)),
+            dma(()),
+            dma(()),
             dma((KV_HEADS,)),
         ],
         compiler_params=pltpu.CompilerParams(

time: 122 us -> 115 us (0.943)
  Pallas kernels: 115 us -> 108 us
    pallas_call x1, Pallas kernels: 115 us -> 108 us  [local(): pl.pallas_call(functools.partial(body, n_groups, n_tp), out_shape=(jax.Sh...]
where the time goes in v6:
time: 115 us
  Pallas kernels  108 us (94%)
  local copies, waits for them, and re-layouts  4.51 us (4%)
  between operations  1.95 us (2%)
    pallas_call x1, Pallas kernels, local(): pl.pallas_call(functools.partial(body, n_groups, n_tp), out_shape=(jax.Sh...  108 us
    unnamed x7, local copies, waits for them, and re-layouts  4.51 us

profile of v6, /device:TPU:8, one launch (start us, length us, event | category | flops | bytes accessed | tf_op | source)
XLA Modules:
  0.0 114.6 jit_solution(6595890638077760651)
XLA Ops:
  1.9 108.1 %shard_map.211 = (bf16[128,8192]{1,0:T(8,128)(2,1)}, bf16[512,128]{1,0:T(8,128)(2,1)}, bf16[32,2,16,128]{3,2,1,0:T(8,128)(2,1)}) custom-call(bf16[128,8192]{1,0:T(8,128)(2,1)} %pq.1, bf16[128,1024]{1,0:T(8,128)(2,1)} %sk.1, bf16[128,1024]{1,0:T(8,128)(2,1)} %sv.1, bf16[128,1024]{1,0:T(8,128)(2,1)} %pk.1, bf16[128,1024]{1,0:T(8,128)(2,1)} %pv.1, ...), custom_call_target="tpu_custom_call" | custom-call | tf_op jit(solution)/shard_map/pallas_call | solution.py:749
  110.1 0.0 copy-start.1
  110.1 0.0 copy-start
  110.1 3.1 %copy.32 = bf16[128,8192]{1,0:T(8,128)(2,1)} copy(bf16[128,8192]{1,0:T(8,128)(2,1)} %get-tuple-element.12) | data formatting | bytes 4194304
  113.2 0.0 copy-done.1
  113.3 0.7 copy.33
  113.9 0.0 copy-done
  113.9 0.7 copy.34
Async XLA Ops:
  110.1 3.2 %copy-start.1 = (bf16[512,128]{1,0:T(8,128)(2,1)S(1)}, bf16[512,128]{1,0:T(8,128)(2,1)}, u32[]{:S(2)}) copy-start(bf16[512,128]{1,0:T(8,128)(2,1)} %get-tuple-element.7) | copy-start | bytes 393220
  110.1 3.8 %copy-start = (bf16[32,2,16,128]{3,2,1,0:T(8,128)(2,1)S(1)}, bf16[32,2,16,128]{3,2,1,0:T(8,128)(2,1)}, u32[]{:S(2)}) copy-start(bf16[32,2,16,128]{3,2,1,0:T(8,128)(2,1)} %get-tuple-element.8) | copy-start | bytes 786436

commit v7 on v6

--- a/solution.py
+++ b/solution.py
@@ -104,7 +104,6 @@
     s_recv,
     b_send,
     b_recv,
-    out_sem,
 ):
     g = lax.axis_index("group")
     t = lax.axis_index("tp")
@@ -170,11 +169,11 @@
     def y_first(i):
         return i % 3 != 1
 
-    def hop(src, dst, kind, i, device):
+    def hop(src, dst, kind, i, device, sent=0):
         return pltpu.make_async_remote_copy(
             src_ref=src,
             dst_ref=dst,
-            send_sem=x_send.at[i, kind],
+            send_sem=x_send.at[i, sent],
             recv_sem=x_recv.at[i, kind],
             device_id=device,
             device_id_type=MESH,
@@ -183,114 +182,67 @@
     def same(ref, kind, i, device):
         return hop(ref, ref, kind, i, device)
 
+    def arrived(ref, kind, i):
+        same(ref, kind, i, to_right).wait_recv()
+
+    def sent(ref, which, i):
+        hop(ref, ref, 0, i, to_right, which).wait_send()
+
     keys, values = pl.ds(0, 2), pl.ds(2, 2)
-
-    def own_right(i, xs):
-        return same(kv.at[i, :, xs, yh], 0, i, to_right)
-
-    def own_left(i, xs):
-        return same(kv.at[i, :, xs, yh], 1, i, to_left)
-
-    def one_y(i, part):
-        rows_of = keys if part == 0 else values
-        device = to_same if part == 0 else to_cross
-        return hop(kv.at[i, rows_of, x, yh], rel.at[i, part, :, 0], 2 + part, i, device)
-
-    def all_y(i, part):
-        rows_of = keys if part == 0 else values
-        device = to_same if part == 0 else to_cross
-        return hop(kv.at[i, rows_of, :, yh], rel.at[i, part], 2 + part, i, device)
-
-    def one_relay(i, part):
-        if part == 0:
-            return hop(rel.at[i, 0, :, 0], kv.at[i, keys, x, yh], 4, i, to_cross)
-        return hop(rel.at[i, 1, :, 0], kv.at[i, values, x, ny], 5, i, to_same)
-
-    def all_relay(i, part):
-        if part == 0:
-            return hop(rel.at[i, 0], kv.at[i, keys, :, yh], 4, i, to_cross)
-        return hop(rel.at[i, 1], kv.at[i, values, :, ny], 5, i, to_same)
-
-    def one_landed(i, part):
-        return same(kv.at[i, (keys, values)[part], x, ny], 4 + part, i, to_same)
-
-    def all_landed(i, part):
-        return same(kv.at[i, (keys, values)[part], :, ny], 4 + part, i, to_same)
-
-    def partner_right(i, xs):
-        return same(kv.at[i, :, xs, ny], 6, i, to_right)
-
-    def partner_left(i, xs):
-        return same(kv.at[i, :, xs, ny], 7, i, to_left)
-
-    def pair_right(i, xs):
-        return same(kv.at[i, keys, xs], 8, i, to_right)
-
-    def pair_left(i, xs):
-        return same(kv.at[i, values, xs], 9, i, to_left)
-
-    def single_right(i, xs):
-        return same(kv.at[i, keys, xs, yh], 8, i, to_right)
-
-    def single_left(i, xs):
-        return same(kv.at[i, values, xs, yh], 9, i, to_left)
 
     def by_kind(i, first, second):
         pl.when(y_first(i))(lambda: first(i))
         pl.when(jnp.logical_not(y_first(i)))(lambda: second(i))
 
     def stage1(i):
+        own = kv.at[i, :, x, yh]
+
         @pl.when(y_first(i))
         def _():
-            one_y(i, 0).start()
-            one_y(i, 1).start()
-
-        own_right(i, x).start()
-        own_left(i, x).start()
+            hop(kv.at[i, keys, x, yh], rel.at[i, 0, :, 0], 2, i, to_same).start()
+            hop(kv.at[i, values, x, yh], rel.at[i, 1, :, 0], 2, i, to_cross).start()
+
+        same(own, 0, i, to_right).start()
+        same(own, 1, i, to_left).start()
 
     def first_a(i):
-        for part in range(2):
-            one_y(i, part).wait_recv()
-            one_relay(i, part).start()
+        arrived(rel.at[i, :, :, 0], 2, i)
+        hop(rel.at[i, 0, :, 0], kv.at[i, keys, x, yh], 3, i, to_cross).start()
+        hop(rel.at[i, 1, :, 0], kv.at[i, values, x, ny], 3, i, to_same).start()
 
     def first_b(i):
-        one_landed(i, 0).wait_recv()
-        one_landed(i, 1).wait_recv()
-        partner_right(i, x).start()
-        partner_left(i, x).start()
+        block = kv.at[i, :, x, ny]
+        arrived(block, 3, i)
+        same(block, 0, i, to_right).start()
+        same(block, 1, i, to_left).start()
 
     def first_c(i):
-        own_right(i, left_x).wait_recv()
-        partner_right(i, left_x).wait_recv()
-        pair_right(i, left_x).start()
-        own_left(i, right_x).wait_recv()
-        partner_left(i, right_x).wait_recv()
-        pair_left(i, right_x).start()
+        arrived(kv.at[i, :, left_x], 0, i)
+        same(kv.at[i, keys, left_x], 4, i, to_right).start()
+        arrived(kv.at[i, :, right_x], 1, i)
+        same(kv.at[i, values, right_x], 4, i, to_left).start()
 
     def first_d(i):
-        pair_right(i, far_x).wait_recv()
-        pair_left(i, far_x).wait_recv()
+        arrived(kv.at[i, :, far_x], 4, i)
 
     def second_a(i):
-        own_right(i, left_x).wait_recv()
-        single_right(i, left_x).start()
-        own_left(i, right_x).wait_recv()
-        single_left(i, right_x).start()
+        arrived(kv.at[i, :, left_x, yh], 0, i)
+        same(kv.at[i, keys, left_x, yh], 4, i, to_right).start()
+        arrived(kv.at[i, :, right_x, yh], 1, i)
+        same(kv.at[i, values, right_x, yh], 4, i, to_left).start()
 
     def second_b(i):
-        single_right(i, far_x).wait_recv()
-        single_left(i, far_x).wait_recv()
-        all_y(i, 0).start()
-        all_y(i, 1).start()
+        arrived(kv.at[i, :, far_x, yh], 4, i)
+        hop(kv.at[i, keys, :, yh], rel.at[i, 0], 2, i, to_same, 1).start()
+        hop(kv.at[i, values, :, yh], rel.at[i, 1], 2, i, to_cross, 1).start()
 
     def second_c(i):
-        for part in range(2):
-            all_y(i, part).wait_recv()
-            all_relay(i, part).start()
+        arrived(rel.at[i], 2, i)
+        hop(rel.at[i, 0], kv.at[i, keys, :, yh], 3, i, to_cross, 1).start()
+        hop(rel.at[i, 1], kv.at[i, values, :, ny], 3, i, to_same, 1).start()
 
     def second_d(i):
-        all_landed(i, 0).wait_recv()
-        all_landed(i, 1).wait_recv()
+        arrived(kv.at[i, :, :, ny], 3, i)
 
     def stage_a(i):
         by_kind(i, first_a, second_a)
@@ -305,24 +257,13 @@
         by_kind(i, first_d, second_d)
 
     def first_drain(i):
-        for part in range(2):
-            one_y(i, part).wait_send()
-            one_relay(i, part).wait_send()
-        partner_right(i, x).wait_send()
-        partner_left(i, x).wait_send()
-        pair_right(i, left_x).wait_send()
-        pair_left(i, right_x).wait_send()
+        sent(kv.at[i], 0, i)
 
     def second_drain(i):
-        for part in range(2):
-            all_y(i, part).wait_send()
-            all_relay(i, part).wait_send()
-        single_right(i, left_x).wait_send()
-        single_left(i, right_x).wait_send()
+        sent(kv.at[i, :, pl.ds(0, 3), 0], 0, i)
+        sent(kv.at[i], 1, i)
 
     def drain_item(i, c):
-        own_right(i, x).wait_send()
-        own_left(i, x).wait_send()
         by_kind(i, first_drain, second_drain)
         return c
 
@@ -620,12 +561,7 @@
             o = o[:, :HEAD_DIM] / o[:, HEAD_DIM:]
             o = jnp.where(live, o, 0.0).astype(jnp.bfloat16)
             for i in range(part):
-                q_s[:, cols(j * part + i)] = o[i * rows : (i + 1) * rows]
-
-    def head_out(h):
-        width = GROUP_SIZE * HEAD_DIM
-        cols = pl.ds(pl.multiple_of(h * width, width), width)
-        return pltpu.make_async_copy(q_s.at[:, cols], p_out.at[:, cols], out_sem.at[h])
+                p_out[:, cols(j * part + i)] = o[i * rows : (i + 1) * rows]
 
     prefill_masks()
     decode()
@@ -639,21 +575,21 @@
     big[2].wait()
 
     def turn(s, c):
+        @pl.when(s + 1 < KV_HEADS)
+        def _():
+            stage_c(s + 1)
+
+        @pl.when(s + 2 < KV_HEADS)
+        def _():
+            stage_b(s + 2)
+
+        @pl.when(s + 3 < KV_HEADS)
+        def _():
+            stage_a(s + 3)
+
         @pl.when(s + window < KV_HEADS)
         def _():
             start_item(s + window, 0)
-
-        @pl.when(s + 3 < KV_HEADS)
-        def _():
-            stage_a(s + 3)
-
-        @pl.when(s + 2 < KV_HEADS)
-        def _():
-            stage_b(s + 2)
-
-        @pl.when(s + 1 < KV_HEADS)
-        def _():
-            stage_c(s + 1)
 
         @pl.when(s == 0)
         def _():
@@ -673,7 +609,6 @@
 
         stage_d(s)
         prefill_head(s)
-        head_out(s).start()
         return c
 
     lax.fori_loop(0, KV_HEADS, turn, 0)
@@ -688,15 +623,10 @@
         ps_copy(h, k).wait_send()
         return c
 
-    def drain_out(h, c):
-        head_out(h).wait()
-        return c
-
     all_msgs().wait_send()
     all_rets().wait_send()
     lax.fori_loop(1, n_tp, drain_tp, 0)
     lax.fori_loop(0, ITEMS, drain_item, 0)
-    lax.fori_loop(0, KV_HEADS, drain_out, 0)
 
 
 def to_rows(queries):
@@ -749,9 +679,9 @@
     p_out, d_out, a_out = pl.pallas_call(
         functools.partial(body, n_groups, n_tp),
         out_shape=(
-            jax.ShapeDtypeStruct(prefill_queries.shape, bf),
-            jax.ShapeDtypeStruct(dq.shape, bf),
-            jax.ShapeDtypeStruct((n_groups, CAPACITY, ROWS16, HEAD_DIM), bf),
+            pltpu.VMEM(prefill_queries.shape, bf),
+            pltpu.VMEM(dq.shape, bf),
+            pltpu.VMEM((n_groups, CAPACITY, ROWS16, HEAD_DIM), bf),
         ),
         in_specs=[any_] * 5
         + [smem] * 2
@@ -760,7 +690,7 @@
         + [vmem] * 3
         + [any_] * 2
         + [vmem] * 3,
-        out_specs=[any_, vmem, vmem],
+        out_specs=[vmem, vmem, vmem],
         scratch_shapes=[
             pltpu.VMEM((ITEMS, 4, X_CHIPS, 2, rows, HEAD_DIM), bf),
             pltpu.VMEM(prefill_queries.shape, bf),
@@ -783,8 +713,8 @@
             pltpu.VMEM((n_groups, CAPACITY, ROWS16, HEAD_DIM), bf),
             dma((KV_HEADS,)),
             dma((5,)),
-            dma((ITEMS, 10)),
-            dma((ITEMS, 10)),
+            dma((ITEMS, 2)),
+            dma((ITEMS, 5)),
             dma(()),
             dma(()),
             dma((n_tp,)),
@@ -793,7 +723,6 @@
             dma((n_tp,)),
             dma(()),
             dma(()),
-            dma((KV_HEADS,)),
         ],
         compiler_params=pltpu.CompilerParams(
             collective_id=0, has_side_effects=True, vmem_limit_bytes=56 * 1024 * 1024

time: 115 us -> 116 us (level)
  Pallas kernels: 108 us -> 110 us
  local copies, waits for them, and re-layouts: 4.51 us -> 2.68 us
    pallas_call x1, Pallas kernels: 108 us -> 110 us  [local(): pl.pallas_call(functools.partial(body, n_groups, n_tp), out_shape=(pltpu....]
    unnamed x7 -> x3, local copies, waits for them, and re-layouts: 4.51 us -> 2.68 us
where the time goes in v7:
time: 116 us; the launch traced here: 115 us
  Pallas kernels  110 us (95%)
  local copies, waits for them, and re-layouts  2.68 us (2%)
  between operations  1.94 us (2%)
    pallas_call x1, Pallas kernels, local(): pl.pallas_call(functools.partial(body, n_groups, n_tp), out_shape=(pltpu....  110 us
    unnamed x3, local copies, waits for them, and re-layouts  2.68 us

profile of v7, /device:TPU:8, one launch (start us, length us, event | category | flops | bytes accessed | tf_op | source)
XLA Modules:
  0.0 115.1 jit_solution(11509267077902644753)
XLA Ops:
  1.9 110.5 %shard_map.211 = (bf16[128,8192]{1,0:T(8,128)(2,1)S(1)}, bf16[512,128]{1,0:T(8,128)(2,1)S(1)}, bf16[32,2,16,128]{3,2,1,0:T(8,128)(2,1)S(1)}) custom-call(bf16[128,8192]{1,0:T(8,128)(2,1)} %pq.1, bf16[128,1024]{1,0:T(8,128)(2,1)} %sk.1, bf16[128,1024]{1,0:T(8,128)(2,1)} %sv.1, bf16[128,1024]{1,0:T(8,128)(2,1)} %pk.1, bf16[128,1024]{1,0:T(8,128)(2,1)} %pv.1, ...), custom_call_target="tpu_custom_call" | custom-call | tf_op jit(solution)/shard_map/pallas_call | solution.py:679
  112.4 1.3 %copy.30 = bf16[128,8192]{1,0:T(8,128)(2,1)} copy(bf16[128,8192]{1,0:T(8,128)(2,1)S(1)} %get-tuple-element.9) | data formatting | bytes 4194304
  113.7 0.7 copy.31
  114.4 0.7 copy.32

commit v8 on v6

--- a/solution.py
+++ b/solution.py
@@ -104,7 +104,6 @@
     s_recv,
     b_send,
     b_recv,
-    out_sem,
 ):
     g = lax.axis_index("group")
     t = lax.axis_index("tp")
@@ -170,11 +169,11 @@
     def y_first(i):
         return i % 3 != 1
 
-    def hop(src, dst, kind, i, device):
+    def hop(src, dst, kind, i, device, sent=0):
         return pltpu.make_async_remote_copy(
             src_ref=src,
             dst_ref=dst,
-            send_sem=x_send.at[i, kind],
+            send_sem=x_send.at[i, sent],
             recv_sem=x_recv.at[i, kind],
             device_id=device,
             device_id_type=MESH,
@@ -199,7 +198,7 @@
     def all_y(i, part):
         rows_of = keys if part == 0 else values
         device = to_same if part == 0 else to_cross
-        return hop(kv.at[i, rows_of, :, yh], rel.at[i, part], 2 + part, i, device)
+        return hop(kv.at[i, rows_of, :, yh], rel.at[i, part], 2 + part, i, device, 1)
 
     def one_relay(i, part):
         if part == 0:
@@ -208,8 +207,8 @@
 
     def all_relay(i, part):
         if part == 0:
-            return hop(rel.at[i, 0], kv.at[i, keys, :, yh], 4, i, to_cross)
-        return hop(rel.at[i, 1], kv.at[i, values, :, ny], 5, i, to_same)
+            return hop(rel.at[i, 0], kv.at[i, keys, :, yh], 4, i, to_cross, 1)
+        return hop(rel.at[i, 1], kv.at[i, values, :, ny], 5, i, to_same, 1)
 
     def one_landed(i, part):
         return same(kv.at[i, (keys, values)[part], x, ny], 4 + part, i, to_same)
@@ -304,25 +303,17 @@
     def stage_d(i):
         by_kind(i, first_d, second_d)
 
+    def sent_all(ref, which, i):
+        hop(ref, ref, 0, i, to_right, which).wait_send()
+
     def first_drain(i):
-        for part in range(2):
-            one_y(i, part).wait_send()
-            one_relay(i, part).wait_send()
-        partner_right(i, x).wait_send()
-        partner_left(i, x).wait_send()
-        pair_right(i, left_x).wait_send()
-        pair_left(i, right_x).wait_send()
+        sent_all(kv.at[i], 0, i)
 
     def second_drain(i):
-        for part in range(2):
-            all_y(i, part).wait_send()
-            all_relay(i, part).wait_send()
-        single_right(i, left_x).wait_send()
-        single_left(i, right_x).wait_send()
+        sent_all(kv.at[i, :, pl.ds(0, 3), 0], 0, i)
+        sent_all(kv.at[i], 1, i)
 
     def drain_item(i, c):
-        own_right(i, x).wait_send()
-        own_left(i, x).wait_send()
         by_kind(i, first_drain, second_drain)
         return c
 
@@ -620,12 +611,7 @@
             o = o[:, :HEAD_DIM] / o[:, HEAD_DIM:]
             o = jnp.where(live, o, 0.0).astype(jnp.bfloat16)
             for i in range(part):
-                q_s[:, cols(j * part + i)] = o[i * rows : (i + 1) * rows]
-
-    def head_out(h):
-        width = GROUP_SIZE * HEAD_DIM
-        cols = pl.ds(pl.multiple_of(h * width, width), width)
-        return pltpu.make_async_copy(q_s.at[:, cols], p_out.at[:, cols], out_sem.at[h])
+                p_out[:, cols(j * part + i)] = o[i * rows : (i + 1) * rows]
 
     prefill_masks()
     decode()
@@ -673,7 +659,6 @@
 
         stage_d(s)
         prefill_head(s)
-        head_out(s).start()
         return c
 
     lax.fori_loop(0, KV_HEADS, turn, 0)
@@ -688,15 +673,10 @@
         ps_copy(h, k).wait_send()
         return c
 
-    def drain_out(h, c):
-        head_out(h).wait()
-        return c
-
     all_msgs().wait_send()
     all_rets().wait_send()
     lax.fori_loop(1, n_tp, drain_tp, 0)
     lax.fori_loop(0, ITEMS, drain_item, 0)
-    lax.fori_loop(0, KV_HEADS, drain_out, 0)
 
 
 def to_rows(queries):
@@ -749,9 +729,9 @@
     p_out, d_out, a_out = pl.pallas_call(
         functools.partial(body, n_groups, n_tp),
         out_shape=(
-            jax.ShapeDtypeStruct(prefill_queries.shape, bf),
-            jax.ShapeDtypeStruct(dq.shape, bf),
-            jax.ShapeDtypeStruct((n_groups, CAPACITY, ROWS16, HEAD_DIM), bf),
+            pltpu.VMEM(prefill_queries.shape, bf),
+            pltpu.VMEM(dq.shape, bf),
+            pltpu.VMEM((n_groups, CAPACITY, ROWS16, HEAD_DIM), bf),
         ),
         in_specs=[any_] * 5
         + [smem] * 2
@@ -760,7 +740,7 @@
         + [vmem] * 3
         + [any_] * 2
         + [vmem] * 3,
-        out_specs=[any_, vmem, vmem],
+        out_specs=[vmem, vmem, vmem],
         scratch_shapes=[
             pltpu.VMEM((ITEMS, 4, X_CHIPS, 2, rows, HEAD_DIM), bf),
             pltpu.VMEM(prefill_queries.shape, bf),
@@ -783,7 +763,7 @@
             pltpu.VMEM((n_groups, CAPACITY, ROWS16, HEAD_DIM), bf),
             dma((KV_HEADS,)),
             dma((5,)),
-            dma((ITEMS, 10)),
+            dma((ITEMS, 2)),
             dma((ITEMS, 10)),
             dma(()),
             dma(()),
@@ -793,7 +773,6 @@
             dma((n_tp,)),
             dma(()),
             dma(()),
-            dma((KV_HEADS,)),
         ],
         compiler_params=pltpu.CompilerParams(
             collective_id=0, has_side_effects=True, vmem_limit_bytes=56 * 1024 * 1024

time: 115 us -> 111 us (0.965)
  Pallas kernels: 108 us -> 106 us
  local copies, waits for them, and re-layouts: 4.51 us -> 2.68 us
    pallas_call x1, Pallas kernels: 108 us -> 106 us  [local(): pl.pallas_call(functools.partial(body, n_groups, n_tp), out_shape=(pltpu....]
    unnamed x7 -> x3, local copies, waits for them, and re-layouts: 4.51 us -> 2.68 us
where the time goes in v8:
time: 111 us
  Pallas kernels  106 us (95%)
  local copies, waits for them, and re-layouts  2.68 us (2%)
  between operations  1.94 us (2%)
    pallas_call x1, Pallas kernels, local(): pl.pallas_call(functools.partial(body, n_groups, n_tp), out_shape=(pltpu....  106 us
    unnamed x3, local copies, waits for them, and re-layouts  2.68 us

profile of v8, /device:TPU:8, one launch (start us, length us, event | category | flops | bytes accessed | tf_op | source)
XLA Modules:
  0.0 110.8 jit_solution(14087421132015214856)
XLA Ops:
  1.9 106.1 %shard_map.211 = (bf16[128,8192]{1,0:T(8,128)(2,1)S(1)}, bf16[512,128]{1,0:T(8,128)(2,1)S(1)}, bf16[32,2,16,128]{3,2,1,0:T(8,128)(2,1)S(1)}) custom-call(bf16[128,8192]{1,0:T(8,128)(2,1)} %pq.1, bf16[128,1024]{1,0:T(8,128)(2,1)} %sk.1, bf16[128,1024]{1,0:T(8,128)(2,1)} %sv.1, bf16[128,1024]{1,0:T(8,128)(2,1)} %pk.1, bf16[128,1024]{1,0:T(8,128)(2,1)} %pv.1, ...), custom_call_target="tpu_custom_call" | custom-call | tf_op jit(solution)/shard_map/pallas_call | solution.py:729
  108.1 1.3 %copy.30 = bf16[128,8192]{1,0:T(8,128)(2,1)} copy(bf16[128,8192]{1,0:T(8,128)(2,1)S(1)} %get-tuple-element.9) | data formatting | bytes 4194304
  109.4 0.7 copy.31
  110.1 0.7 copy.32

commit v9 on v8

--- a/solution.py
+++ b/solution.py
@@ -614,10 +614,11 @@
                 p_out[:, cols(j * part + i)] = o[i * rows : (i + 1) * rows]
 
     prefill_masks()
+    stage_a(0)
+    stage_a(2)
     decode()
-    for h in range(3):
-        stage_a(h)
     stage_b(0)
+    stage_a(1)
     arrivals_choose()
     stage_b(1)
     stage_c(0)

time: 111 us -> 111 us (level)
  no operation moved by 1% of the time
where the time goes in v9:
time: 111 us
  Pallas kernels  106 us (95%)
  local copies, waits for them, and re-layouts  2.68 us (2%)
  between operations  1.94 us (2%)
    pallas_call x1, Pallas kernels, local(): pl.pallas_call(functools.partial(body, n_groups, n_tp), out_shape=(pltpu....  106 us
    unnamed x3, local copies, waits for them, and re-layouts  2.68 us

profile of v9, /device:TPU:8, one launch (start us, length us, event | category | flops | bytes accessed | tf_op | source)
XLA Modules:
  0.0 111.0 jit_solution(1340668441153848039)
XLA Ops:
  1.9 106.4 %shard_map.211 = (bf16[128,8192]{1,0:T(8,128)(2,1)S(1)}, bf16[512,128]{1,0:T(8,128)(2,1)S(1)}, bf16[32,2,16,128]{3,2,1,0:T(8,128)(2,1)S(1)}) custom-call(bf16[128,8192]{1,0:T(8,128)(2,1)} %pq.1, bf16[128,1024]{1,0:T(8,128)(2,1)} %sk.1, bf16[128,1024]{1,0:T(8,128)(2,1)} %sv.1, bf16[128,1024]{1,0:T(8,128)(2,1)} %pk.1, bf16[128,1024]{1,0:T(8,128)(2,1)} %pv.1, ...), custom_call_target="tpu_custom_call" | custom-call | tf_op jit(solution)/shard_map/pallas_call | solution.py:730
  108.3 1.3 %copy.30 = bf16[128,8192]{1,0:T(8,128)(2,1)} copy(bf16[128,8192]{1,0:T(8,128)(2,1)S(1)} %get-tuple-element.9) | data formatting | bytes 4194304
  109.6 0.7 copy.31
  110.3 0.7 copy.32
